TPU v7x, 256 devices: a whole 4x4x8 slice. The times are simulated.
256 devices in a mesh: seq: 8 (over z_hi, core), fsdp: 32 (over x, y, z_lo).
Axes of the slice: x: 4, y: 4, z: 8 (z_hi: 4, z_lo: 2; z = z_hi * 2 + z_lo), core: 2. Of those that a mesh axis runs over, the one named last changes fastest.
Arguments:
- tokens: bfloat16 [32, 2, 1024, 1024], P('fsdp', None, 'seq'), may hold values from -6 to 6
- proj: bfloat16 [1024, 3, 512], P('fsdp'), may hold values from -0.1875 to 0.1875
- state: float32 [32, 2, 3, 256, 512], P('fsdp'), may hold values from -0.375 to 0.375
- step_rates: float32 [32, 2, 1024], P('fsdp', None, 'seq'), may hold values from 0.00048828125 to 0.0048828125
- d_out: bfloat16 [32, 2, 1024, 512], P('fsdp', None, 'seq'), may hold values from -6 to 6
Outputs:
- d_tokens: bfloat16 [32, 2, 1024, 1024], P('fsdp', None, 'seq')
- d_state: float32 [32, 2, 3, 256, 512], P('fsdp', None, None, 'seq')
- d_proj: float32 [1024, 3, 512], P('fsdp')
All inputs are finite; a program needn't handle non-finite values.
Results may differ from a plain program's by a relative error of at most 0.04.
Values may be sent and summed in bfloat16 or wider, within the bound.
No kernel may reach another device: no remote copies, remote signals or barrier semaphores. Data moves between devices by JAX's collectives and lax.ppermute only.
A program may use at most 128 MiB of HBM per device.

v0:
```python
from functools import partial

import jax
import jax.numpy as jnp
from jax import lax
from jax.sharding import PartitionSpec as P

HIGH = lax.Precision.HIGHEST
EPS = 1e-06


def unit_rows(values):
    return values * lax.rsqrt(jnp.mean(values * values, axis=-1, keepdims=True) + EPS)


def fast_apply(weights, inputs):
    gate_part = jnp.einsum("rhd,hdm->rhm", inputs, weights[:, 0], precision=HIGH)
    up_part = jnp.einsum("rhd,hdm->rhm", inputs, weights[:, 1], precision=HIGH)
    hidden = jax.nn.silu(gate_part) * up_part
    return jnp.einsum("rhm,hdm->rhd", hidden, weights[:, 2], precision=HIGH)


def update_term(learn_rate, weights, key_rows, values):

    def objective(current):
        return jnp.sum(fast_apply(current, unit_rows(key_rows)) * values * learn_rate[:, :, None])

    return jax.grad(objective)(weights)


def first_span(learn_rate, weights, queries, key_rows, values):
    return (
        fast_apply(weights, unit_rows(queries)),
        update_term(learn_rate, weights, key_rows, values),
    )


def second_span(weights, queries):
    return fast_apply(weights, unit_rows(queries))


def on_device(tokens, proj, state, step_rates, d_out):
    tok_count = tokens.shape[2]
    model_width = tokens.shape[3]
    head_count = state.shape[1]
    head_dim = state.shape[3]
    inner_width = head_count * head_dim
    owned_rows = proj.shape[0]
    flat_tokens = tokens.reshape(2 * tok_count, model_width)
    gathered = lax.all_gather(proj, "fsdp", axis=0, tiled=True)
    flat_whole = gathered.reshape(model_width, 3 * inner_width)
    packed = jnp.dot(flat_tokens, flat_whole, preferred_element_type=jnp.float32)
    rounded = lax.optimization_barrier(packed.astype(jnp.bfloat16))
    projected = rounded.astype(jnp.float32).reshape(2, tok_count, 3, head_count, head_dim)
    cotangent = d_out.astype(jnp.float32).reshape(2, tok_count, head_count, head_dim)
    start_state = state[0]
    learn_rate = step_rates[0].T
    early_out, early_pull = jax.vjp(
        partial(first_span, learn_rate),
        start_state,
        projected[0, :, 0],
        projected[0, :, 1],
        projected[0, :, 2],
    )
    next_state = start_state + lax.psum(early_out[1].astype(jnp.bfloat16), "seq").astype(
        jnp.float32
    )
    _, late_pull = jax.vjp(second_span, next_state, projected[1, :, 0])
    late_state, late_query = late_pull(cotangent[1])
    carried = lax.psum(late_state.astype(jnp.bfloat16), "seq").astype(jnp.float32)
    early_state, early_query, early_key, early_value = early_pull((cotangent[0], carried))
    share_rows = head_dim // lax.axis_size("seq")
    local_grad = lax.psum_scatter(
        early_state.astype(jnp.bfloat16), "seq", scatter_dimension=2, tiled=True
    ).astype(jnp.float32)
    own_carried = lax.dynamic_slice_in_dim(
        carried, lax.axis_index("seq") * share_rows, share_rows, 2
    )
    state_grad = (own_carried + local_grad)[None]
    early_grad = jnp.stack([early_query, early_key, early_value], axis=1)
    late_grad = jnp.concatenate([late_query[:, None], jnp.zeros_like(early_grad[:, 1:])], axis=1)
    grad_parts = (
        jnp.stack([early_grad, late_grad])
        .astype(jnp.bfloat16)
        .reshape(2 * tok_count, 3 * inner_width)
    )
    grad_tokens = lax.dot_general(
        grad_parts, flat_whole, (((1,), (1,)), ((), ())), preferred_element_type=jnp.float32
    )
    d_tokens = grad_tokens.astype(jnp.bfloat16).reshape(1, 2, tok_count, model_width)
    owner_sum = lax.psum_scatter(
        lax.dot_general(
            flat_tokens, grad_parts, (((0,), (0,)), ((), ())), preferred_element_type=jnp.float32
        ).astype(jnp.bfloat16),
        "fsdp",
        scatter_dimension=0,
        tiled=True,
    )
    proj_grad = lax.psum(owner_sum, "seq").astype(jnp.float32).reshape(owned_rows, 3, inner_width)
    return (d_tokens, state_grad, proj_grad)


def solution(mesh):
    placed = (
        P("fsdp", None, "seq", None),
        P("fsdp", None, None),
        P("fsdp", None, None, None, None),
        P("fsdp", None, "seq"),
        P("fsdp", None, "seq", None),
    )
    return jax.shard_map(
        on_device,
        mesh=mesh,
        in_specs=placed,
        out_specs=(
            P("fsdp", None, "seq", None),
            P("fsdp", None, None, "seq", None),
            P("fsdp", None, None),
        ),
        check_vma=False,
    )
```

profile of v0, /device:TPU:1, one launch (start us, length us, event | category | flops | bytes accessed | tf_op | source)
XLA Modules:
  0.0 649.1 jit_solution(13499650306375668626)
XLA Ops:
  8.0 4.2 copy.328
  12.4 2.6 fusion.14
  15.0 143.3 %all-gather.2.cloned.1.call-done = bf16[1024,3,512]{2,0,1:T(8,128)(2,1)} async-done(((bf16[32,3,512]{2,0,1:T(8,128)(2,1)}), bf16[1024,3,512]{2,0,1:T(8,128)(2,1)}) %all-gather.2.cloned.1.call-update) | async-done | bytes 3145744 | tf_op jit(solution)/shard_map/all_gather | solution.py:50
  158.3 4.6 copy.146
  162.9 2.9 convolution_convert_fusion.1
  167.3 2.2 fusion.17
  174.6 1.5 add_convert_fusion.2
  176.6 2.1 fusion.16
  178.7 2.2 fusion.18
  182.2 2.1 multiply_reduce_fusion.4
  184.3 90.5 %all-reduce.19.cloned.1.call-done = bf16[2,3,256,512]{3,2,0,1:T(8,128)(2,1)} async-done(((bf16[2,3,256,512]{3,2,0,1:T(8,128)(2,1)}), bf16[2,3,256,512]{3,2,0,1:T(8,128)(2,1)}) %all-reduce.19.cloned.1.call-update) | async-done | bytes 1572880 | tf_op jit(solution)/shard_map/psum | solution.py:65
  274.8 2.9 convert_add_fusion
  285.7 2.7 fusion.12
  288.4 2.7 multiply_reduce_fusion
  291.3 73.0 %all-reduce.21.cloned.1.call-done = bf16[2,3,256,512]{2,3,0,1:T(8,128)(2,1)} async-done(((bf16[2,3,256,512]{2,3,0,1:T(8,128)(2,1)}), bf16[2,3,256,512]{2,3,0,1:T(8,128)(2,1)}) %all-reduce.21.cloned.1.call-update) | async-done | bytes 1572880 | tf_op jit(solution)/shard_map/psum | solution.py:70
  364.3 1.8 fusion.55
  366.2 2.1 fusion.33
  377.2 2.7 fusion
  379.9 4.7 copy.257
  386.5 2.3 convolution_bitcast_fusion.1
  394.2 2.8 copy.210
  397.0 136.8 %reduce-scatter.4.cloned.1.call-done = bf16[32,1536]{1,0:T(8,128)(2,1)} async-done(((bf16[1024,1536]{1,0:T(8,128)(2,1)}), bf16[32,1536]{1,0:T(8,128)(2,1)}) %reduce-scatter.4.cloned.1.call-update) | async-done | bytes 98320
  537.0 3.7 convolution_convert_fusion.2
  540.6 96.7 %all-reduce.23.cloned.1.call-done = (bf16[2,3,256,512]{3,0,1,2:T(2,128)(2,1)}, bf16[32,3,512]{2,0,1:T(8,128)(2,1)}) async-done(((bf16[2,3,256,512]{3,0,1,2:T(2,128)(2,1)}, bf16[32,3,512]{2,0,1:T(8,128)(2,1)}), (bf16[2,3,256,512]{3,0,1,2:T(2,128)(2,1)}, bf16[32,3,512]{2,0,1:T(8,128)(2,1)})) %all-reduce.23.cloned.1.call-update) | async-done | bytes 1671184
  (136 shorter events, 40.5 us)
Async XLA Ops:
  7.2 155.8 %copy-start = (bf16[1,2,128,1024]{3,2,1,0:T(8,128)(2,1)S(1)}, bf16[1,2,128,1024]{3,2,1,0:T(8,128)(2,1)}, u32[]{:S(2)}) copy-start(bf16[1,2,128,1024]{3,2,1,0:T(8,128)(2,1)} %param.5) | copy-start | bytes 1572868
  7.2 151.1 %all-gather.2.cloned.1.call-start = ((), (), s32[]{:S(2)}) async-start(), calls=%async_computation.1 | async-start | bytes 3244032 | tf_op jit(solution)/shard_map/all_gather | solution.py:50
  7.9 4.2 copy-start.31
  7.9 266.8 %all-reduce.19.cloned.1.call-start = ((), (), s32[]{:S(2)}) async-start(), calls=%async_computation.2 | async-start | bytes 3145728 | tf_op jit(solution)/shard_map/psum | solution.py:65
  166.8 3.5 copy-start.33
  169.6 3.9 copy-start.18
  176.1 4.8 copy-start.27
  176.1 188.2 %all-reduce.21.cloned.1.call-start = ((), (), s32[]{:S(2)}) async-start(), calls=%async_computation.3 | async-start | bytes 3145728 | tf_op jit(solution)/shard_map/psum | solution.py:70
  176.3 4.6 copy-start.2
  178.7 5.6 copy-start.12
  284.2 4.1 copy-start.26
  284.3 249.5 %reduce-scatter.4.cloned.1.call-start = ((), (), s32[]{:S(2)}) async-start(), calls=%async_computation.4 | async-start | bytes 3244032
  284.5 3.9 copy-start.30
  288.4 77.7 %copy-start.19 = (f32[2,128,512]{2,1,0:T(8,128)S(1)}, f32[2,128,512]{2,1,0:T(8,128)}, u32[]{:S(2)}) copy-start(f32[2,128,512]{2,1,0:T(8,128)} %copy-done.18) | copy-start | bytes 1572868
  364.3 4.8 copy-start.3
  366.1 4.1 copy-start.11
  366.1 4.1 copy-start.20
  366.1 4.1 copy-start.22
  366.2 4.1 copy-start.24
  384.6 252.8 %all-reduce.23.cloned.1.call-start = ((), (), s32[]{:S(2)}) async-start(), calls=%async_computation.5 | async-start | bytes 3342336
  386.5 3.5 copy-start.10
  386.5 4.6 copy-start.8
  388.8 3.4 copy-start.6
  394.2 141.5 %copy-start.34 = (u32[256]{0:T(256)S(1)}, u32[256]{0:T(256)}, u32[]{:S(2)}) copy-start(u32[256]{0:T(256)} %constant.67) | copy-start | bytes 3076
  (16 other events, 40.7 us)
Sparse Core Ops, SparseCore 0:
  9.8 148.4 all-gather.1
  176.2 98.4 all-reduce.18
  284.4 79.8 all-reduce.20
  384.7 149.0 reduce-scatter.3
  537.2 100.1 all-reduce.22
where the time goes:
time: 656 us; the launch traced here: 649 us
  waiting for transfers between devices  541 us (82%)
  matrix products  54.8 us (8%)
  local copies, waits for them, and re-layouts  26.1 us (4%)
  between operations  15.7 us (2%)
  other arithmetic  10.7 us (2%)
    unnamed x7, waiting for transfers between devices  234 us
    all_gather x1, waiting for transfers between devices, on_device(): gathered = lax.all_gather(proj, 'fsdp', axis=0, tiled=True)  143 us
    psum x1, waiting for transfers between devices, on_device(): lax.psum(early_out[1].astype(jnp.bfloat16), 'seq').astype(jnp.float32)  90.5 us
    psum x1, waiting for transfers between devices, on_device(): lax.psum(late_state.astype(jnp.bfloat16), 'seq').astype(jnp.float32)  73 us
    dot_general x12, matrix products, fast_apply(): up_part = jnp.einsum('rhd,hdm->rhm', inputs, weights[:, 1], precision=HIGH)  18.6 us
    dot_general x12, matrix products, fast_apply(): jnp.einsum('rhd,hdm->rhm', inputs, weights[:, 0], precision=HIGH)  16.6 us
    unnamed x76, local copies, waits for them, and re-layouts  14.6 us
  transfers between devices with their start and end apart: 5, of which 5 were waited for; matrix products, arithmetic and copies ran while one was open for 6% of the time, Pallas kernels for 0%

commit v1 on v0

v1 whole, which is shorter than its diff:
```python
from functools import partial

import jax
import jax.numpy as jnp
from jax import lax
from jax.experimental import pallas as pl
from jax.experimental.pallas import tpu as pltpu
from jax.sharding import PartitionSpec as P

EPS = 1e-06
BF = jnp.bfloat16
F32 = jnp.float32
CORES = 2


def dot_nn(a, b):
    return lax.dot_general(a, b, (((1,), (0,)), ((), ())), preferred_element_type=F32)


def dot_nt(a, b):
    return lax.dot_general(a, b, (((1,), (1,)), ((), ())), preferred_element_type=F32)


def dot_tn(a, b):
    return lax.dot_general(a, b, (((0,), (0,)), ((), ())), preferred_element_type=F32)


def inverse_rms(values):
    return lax.rsqrt(jnp.mean(values * values, axis=-1, keepdims=True) + EPS)


def unit_pull(grad, unit, scale):
    return scale * (grad - unit * jnp.mean(grad * unit, axis=-1, keepdims=True))


def as_column(row):
    count = row.shape[1]
    eye = lax.broadcasted_iota(jnp.int32, (count, count), 0) == lax.broadcasted_iota(
        jnp.int32, (count, count), 1
    )
    return jnp.sum(jnp.where(eye, row, 0.0), axis=1, keepdims=True)


def hidden_parts(unit, cot, weights):
    gate = dot_nn(unit, weights[0])
    up = dot_nn(unit, weights[1])
    back = dot_nn(cot, weights[2])
    sig = 0.5 * jnp.tanh(0.5 * gate) + 0.5
    act = gate * sig
    slope = sig + act * (1.0 - sig)
    return gate, up, back, sig, act, slope


def weight_terms(unit, cot, weights):
    gate, up, back, sig, act, slope = hidden_parts(unit, cot, weights)
    d_up = (back * act).astype(BF)
    d_gate = (back * up * slope).astype(BF)
    hidden = (act * up).astype(BF)
    return d_gate, d_up, hidden


def update_kernel(count, *refs):
    tok = refs[: 2 * count]
    proj, state, rates, cot0, cot0_mate = refs[2 * count : 2 * count + 5]
    next_ref, kv_ref, early_ref, dq_ref = refs[2 * count + 5 : 2 * count + 9]
    keys, w16, total = refs[2 * count + 9 :]
    rows = tok[0].shape[0]
    dim = state.shape[1]
    span = 2 * rows
    for part in range(3):
        w16[part] = state[part].astype(BF)
    weights = (w16[0], w16[1], w16[2])
    own = jnp.concatenate([tok[0][...], tok[1][...]], axis=0)
    query = dot_nn(own, proj[:, :dim]).astype(BF).astype(F32)
    scale = inverse_rms(query)
    unit = query * scale
    unit16 = unit.astype(BF)
    cot = jnp.concatenate([cot0[...], cot0_mate[...]], axis=0)
    d_gate, d_up, hidden = weight_terms(unit16, cot, weights)
    early_ref[0] = dot_tn(unit16, d_gate)
    early_ref[1] = dot_tn(unit16, d_up)
    early_ref[2] = dot_tn(cot, hidden)
    pulled = dot_nt(d_gate, weights[0]) + dot_nt(d_up, weights[1])
    dq_ref[...] = unit_pull(pulled, unit, scale).astype(BF)

    for block in range(count):
        both = jnp.concatenate([tok[2 * block][...], tok[2 * block + 1][...]], axis=0)
        keys[pl.ds(block * span, span), :] = dot_nn(both, proj[:, dim:]).astype(BF)
    kv_ref[...] = keys[pl.ds(0, span), :]
    for part in range(3):
        total[part] = state[part]

    def step(block, carry):
        pair = keys[pl.ds(pl.multiple_of(block * span, span), span), :].astype(F32)
        rate = jnp.concatenate(
            [as_column(rates[pl.ds(2 * block + half, 1), :]) for half in range(2)], axis=0
        )
        key = pair[:, :dim]
        unit16 = (key * inverse_rms(key)).astype(BF)
        cot = (pair[:, dim:] * rate).astype(BF)
        d_gate, d_up, hidden = weight_terms(unit16, cot, (w16[0], w16[1], w16[2]))
        total[0] += dot_tn(unit16, d_gate)
        total[1] += dot_tn(unit16, d_up)
        total[2] += dot_tn(cot, hidden)
        return carry

    lax.fori_loop(0, count, step, 0)
    for part in range(3):
        next_ref[part] = total[part].astype(BF)


def late_kernel(count, place, *refs):
    queries = refs[:count]
    cots = refs[count : 2 * count]
    (next_w, state, rates, kv, early, dq0, tok0, tok0_mate, tok1, tok1_mate) = refs[
        2 * count : 2 * count + 10
    ]
    (own_ref, share_ref, dproj_ref, g0_ref, g1_ref) = refs[2 * count + 10 : 2 * count + 15]
    w16, c16, units, total = refs[2 * count + 15 :]
    span, dim = kv.shape[0], state.shape[1]
    share = dim // count
    for part in range(3):
        w16[part] = state[part].astype(BF)
        total[part] = jnp.zeros_like(total[part])
    late = (next_w[0], next_w[1], next_w[2])
    for block in range(count):
        query = queries[block][...].astype(F32)
        scale = inverse_rms(query)
        unit = query * scale
        unit16 = unit.astype(BF)
        cot = cots[block][...]
        d_gate, d_up, hidden = weight_terms(unit16, cot, late)
        total[0] += dot_tn(unit16, d_gate)
        total[1] += dot_tn(unit16, d_up)
        total[2] += dot_tn(cot, hidden)
        if block == 0:
            pulled = dot_nt(d_gate, late[0]) + dot_nt(d_up, late[1])
            g1_ref[...] = unit_pull(pulled, unit, scale).astype(BF)
    for part in range(3):
        c16[part] = total[part].astype(BF)
    start = pl.multiple_of(place[0] * share, share)
    for part in range(3):
        own_ref[part] = total[part, pl.ds(start, share), :]

    pair = kv[...].astype(F32)
    key, value = pair[:, :dim], pair[:, dim:]
    rate = jnp.concatenate([as_column(rates[half : half + 1, :]) for half in range(2)], axis=0)
    scale = inverse_rms(key)
    unit = key * scale
    unit16 = unit.astype(BF)
    cot = (value * rate).astype(BF)
    gate, up, back, sig, act, slope = hidden_parts(unit16, cot, (w16[0], w16[1], w16[2]))
    curve = sig * (1.0 - sig) * (2.0 + gate * (1.0 - 2.0 * sig))
    gate_dot = dot_nn(unit16, c16[0])
    up_dot = dot_nn(unit16, c16[1])
    back_dot = dot_nn(cot, c16[2])
    d_up1 = (back * act).astype(BF)
    d_gate1 = (back * up * slope).astype(BF)
    hidden = (act * up).astype(BF)
    slope_dot = slope * gate_dot
    hidden_dot = (slope_dot * up + act * up_dot).astype(BF)
    d_gate = (back * (curve * gate_dot * up + slope * up_dot) + back_dot * slope * up).astype(BF)
    d_up = (back * slope_dot + back_dot * act).astype(BF)
    d_value = rate * (dot_nt(hidden_dot, w16[2]) + dot_nt(hidden, c16[2]))
    d_unit = (
        dot_nt(d_gate, w16[0])
        + dot_nt(d_up, w16[1])
        + dot_nt(d_gate1, c16[0])
        + dot_nt(d_up1, c16[1])
    )
    g0_ref[:, :dim] = dq0[...]
    g0_ref[:, dim : 2 * dim] = unit_pull(d_unit, unit, scale).astype(BF)
    g0_ref[:, 2 * dim :] = d_value.astype(BF)
    total[0] = early[0] + dot_tn(unit16, d_gate)
    total[1] = early[1] + dot_tn(unit16, d_up)
    total[2] = early[2] + dot_tn(cot, hidden_dot)
    for other in range(count):
        at = lax.rem(place[0] + other, count)
        at = pl.multiple_of(at * share, share)
        for part in range(3):
            share_ref[other, part] = total[part, pl.ds(at, share), :].astype(BF)

    width = tok0.shape[1]
    columns = 256

    def project(step, carry):
        at = pl.ds(pl.multiple_of(step * columns, columns), columns)
        first = jnp.concatenate([tok0[:, at], tok0_mate[:, at]], axis=0)
        second = jnp.concatenate([tok1[:, at], tok1_mate[:, at]], axis=0)
        out = dot_tn(first, g0_ref[...])
        extra = dot_tn(second, g1_ref[...])
        dproj_ref[at, :dim] = (out[:, :dim] + extra).astype(BF)
        dproj_ref[at, dim:] = out[:, dim:].astype(BF)
        return carry

    lax.fori_loop(0, width // columns, project, 0)


VMEM = pl.BlockSpec(memory_space=pltpu.VMEM)
SMEM = pl.BlockSpec(memory_space=pltpu.SMEM)


def on_device(groups, tokens, proj, state, step_rates, d_out):
    rows, width = tokens.shape[2:]
    heads, _, dim, hid = state.shape[1:]
    owned = proj.shape[0]
    peers = groups
    span = CORES * rows
    spot = lax.axis_index("seq")
    core = lax.rem(spot, CORES)
    place = spot // CORES

    def to_mate(value):
        return lax.ppermute(
            value, "seq", [(i, (i // CORES) * CORES + (i + 1) % CORES) for i in range(groups * CORES)]
        )

    def along(value, hop):
        return lax.ppermute(
            value,
            "seq",
            [(i, ((i // CORES + hop) % groups) * CORES + i % CORES) for i in range(groups * CORES)],
        )

    hops = range(1, groups)

    def mine(value):
        half = value.shape[-1] // CORES
        return jnp.where(core == 0, value[..., :half], value[..., half:])

    def other(value):
        half = value.shape[-1] // CORES
        return jnp.where(core == 0, value[..., half:], value[..., :half])

    tok = tokens[0]
    tok_mate = to_mate(tok)
    pieces = [tok[0], tok_mate[0]]
    far = [along(tok[0], hop) for hop in hops]
    for item in far:
        pieces += [item, to_mate(item)]
    cot = mine(d_out[0])
    cot_mate = to_mate(other(d_out[0]))
    cot1 = jnp.concatenate([cot[1], cot_mate[1]], axis=0)
    cots = [cot1] + [along(cot1, hop) for hop in hops]
    rate = step_rates[0]
    all_rates = jnp.stack([rate] + [along(rate, hop) for hop in hops])
    rate_mine = jnp.where(core == 0, all_rates[:, 0], all_rates[:, 1])
    rate_mate = to_mate(jnp.where(core == 0, all_rates[:, 1], all_rates[:, 0]))
    rates = jnp.stack([rate_mine, rate_mate], axis=1).reshape(groups * CORES, rows)

    proj_mine = mine(proj).reshape(1, owned, 3 * dim)
    devices = lax.axis_size("fsdp")
    whole = lax.all_to_all(
        jnp.broadcast_to(proj_mine, (devices, owned, 3 * dim)), "fsdp", 0, 0, tiled=True
    ).reshape(devices * owned, 3 * dim)
    own_state = jnp.where(core == 0, state[0, 0], state[0, 1])

    second = jnp.concatenate([tok[1], tok_mate[1]], axis=0)
    query1 = jnp.dot(second, whole[:, :dim], preferred_element_type=F32).astype(BF)
    queries = [query1] + [along(query1, hop) for hop in hops]

    shape = jax.ShapeDtypeStruct
    params = pltpu.CompilerParams(vmem_limit_bytes=56 * 2**20)
    next16, kv, early, dq0 = pl.pallas_call(
        partial(update_kernel, groups),
        out_shape=(
            shape((3, dim, hid), BF),
            shape((span, 2 * dim), BF),
            shape((3, dim, hid), F32),
            shape((span, dim), BF),
        ),
        in_specs=[VMEM] * (2 * groups + 5),
        out_specs=(VMEM,) * 4,
        scratch_shapes=[
            pltpu.VMEM((groups * span, 2 * dim), BF),
            pltpu.VMEM((3, dim, hid), BF),
            pltpu.VMEM((3, dim, hid), F32),
        ],
        compiler_params=params,
        name="update",
    )(*pieces, whole, own_state, rates, cot[0], cot_mate[0])

    share = dim // groups
    carried, shares, dproj, grads0, grads1 = pl.pallas_call(
        partial(late_kernel, groups),
        out_shape=(
            shape((3, share, hid), F32),
            shape((groups, 3, share, hid), BF),
            shape((width, 3 * dim), BF),
            shape((span, 3 * dim), BF),
            shape((span, dim), BF),
        ),
        in_specs=[SMEM] + [VMEM] * (2 * groups + 10),
        out_specs=(VMEM,) * 5,
        scratch_shapes=[
            pltpu.VMEM((3, dim, hid), BF),
            pltpu.VMEM((3, dim, hid), BF),
            pltpu.VMEM((8, 128), F32),
            pltpu.VMEM((3, dim, hid), F32),
        ],
        compiler_params=params,
        name="late",
    )(
        place.reshape(1).astype(jnp.int32),
        *queries,
        *cots,
        next16,
        own_state,
        rates,
        kv,
        early,
        dq0,
        tok[0],
        tok_mate[0],
        tok[1],
        tok_mate[1],
    )

    swapped = lax.all_to_all(dproj.reshape(devices, owned, 3 * dim), "fsdp", 0, 0, tiled=True)
    owner = jnp.sum(swapped.astype(F32), axis=0).astype(BF)
    owner_all = owner.astype(F32)
    for hop in hops:
        owner_all = owner_all + along(owner, hop).astype(F32)
    owner_mate = to_mate(owner_all)
    owner_all = owner_all.reshape(owned, 3, dim)
    owner_mate = owner_mate.reshape(owned, 3, dim)
    d_proj = jnp.where(
        core == 0,
        jnp.concatenate([owner_all, owner_mate], axis=-1),
        jnp.concatenate([owner_mate, owner_all], axis=-1),
    )

    summed = carried + shares[0].astype(F32)
    for hop in hops:
        summed = summed + along(shares[hop], hop).astype(F32)
    half = share // CORES
    keep = jnp.where(core == 0, summed[:, :half], summed[:, half:])
    give = jnp.where(core == 0, summed[:, half:], summed[:, :half])
    got = to_mate(give)
    d_state = jnp.where(core == 0, jnp.stack([keep, got]), jnp.stack([got, keep]))[None]

    part0 = lax.dot_general(
        grads0, whole, (((1,), (1,)), ((), ())), preferred_element_type=F32
    )
    part1 = lax.dot_general(
        grads1, whole[:, :dim], (((1,), (1,)), ((), ())), preferred_element_type=F32
    )
    part = jnp.stack([part0, part1])
    from_mate = to_mate(part[:, rows:].astype(BF))
    d_tokens = (part[:, :rows] + from_mate.astype(F32)).astype(BF)[None]
    return (d_tokens, d_state, d_proj)


def solution(mesh):
    groups = mesh.shape["seq"] // CORES
    placed = (
        P("fsdp", None, "seq", None),
        P("fsdp", None, None),
        P("fsdp", None, None, None, None),
        P("fsdp", None, "seq"),
        P("fsdp", None, "seq", None),
    )
    return jax.shard_map(
        partial(on_device, groups),
        mesh=mesh,
        in_specs=placed,
        out_specs=(
            P("fsdp", None, "seq", None),
            P("fsdp", None, None, "seq", None),
            P("fsdp", None, None),
        ),
        check_vma=False,
    )
```

time: 656 us -> 160 us (0.24)
  waiting for transfers between devices: 541 us -> 41.1 us
  starting transfers between devices: 0.84 us -> 79.7 us
  matrix products: 54.8 us -> 1.23 us
  local copies, waits for them, and re-layouts: 26.1 us -> 5.69 us
  Pallas kernels: 0 us -> 20 us
  between operations: 15.7 us -> 1.06 us
    unnamed x7 -> x0, waiting for transfers between devices: 234 us -> none
    psum x2 -> x0, waiting for transfers between devices: 163 us -> none  [the longest x1 90.5 us: on_device(): lax.psum(early_out[1].astype(jnp.bfloat16), 'seq').astype(jnp.float32)]
    all_gather x1 -> x0, waiting for transfers between devices: 143 us -> none  [on_device(): gathered = lax.all_gather(proj, 'fsdp', axis=0, tiled=True)]
    ppermute x0 -> x27, starting transfers between devices: none -> 57.7 us  [the longest x18 44.3 us: along(): lax.ppermute(value, 'seq', [(i, (i // CORES + hop) % groups * CORES + i %...]
    dot_general x37 -> x3, matrix products: 54.8 us -> 1.23 us  [the longest x1 0.6 us: on_device(): lax.dot_general(grads0, whole, (((1,), (1,)), ((), ())), preferred_elemen...]
    ppermute x0 -> x27, waiting for transfers between devices: none -> 41.1 us  [the longest x18 41.1 us: along(): lax.ppermute(value, 'seq', [(i, (i // CORES + hop) % groups * CORES + i %...]
    all_to_all x0 -> x2, starting transfers between devices: none -> 22 us  [the longest x1 12.6 us: on_device(): lax.all_to_all(dproj.reshape(devices, owned, 3 * dim), 'fsdp', 0, 0, tile...]
    pallas_call x0 -> x2, Pallas kernels: none -> 20 us  [the longest x1 10.5 us: on_device(): pl.pallas_call(partial(late_kernel, groups), out_shape=(shape((3, share,...]
  transfers between devices with their start and end apart: 5 -> 29, of which waited for: 5 -> 7; matrix products, arithmetic and copies ran while one was open for 6% -> 9% of each run, Pallas kernels for 0% -> 6%
where the time goes in v1:
time: 160 us; the launch traced here: 159 us
  starting transfers between devices  79.7 us (50%)
  waiting for transfers between devices  41.1 us (26%)
  Pallas kernels  20 us (12%)
  other arithmetic  10.5 us (7%)
  local copies, waits for them, and re-layouts  5.69 us (4%)
    ppermute x18, starting transfers between devices, along(): lax.ppermute(value, 'seq', [(i, (i // CORES + hop) % groups * CORES + i %...  44.3 us
    ppermute x18, waiting for transfers between devices, along(): lax.ppermute(value, 'seq', [(i, (i // CORES + hop) % groups * CORES + i %...  41.1 us
    ppermute x9, starting transfers between devices, to_mate(): lax.ppermute(value, 'seq', [(i, i // CORES * CORES + (i + 1) % CORES) for...  13.4 us
    all_to_all x1, starting transfers between devices, on_device(): lax.all_to_all(dproj.reshape(devices, owned, 3 * dim), 'fsdp', 0, 0, tile...  12.6 us
    pallas_call x1, Pallas kernels, on_device(): pl.pallas_call(partial(late_kernel, groups), out_shape=(shape((3, share,...  10.5 us
    pallas_call x1, Pallas kernels, on_device(): pl.pallas_call(partial(update_kernel, groups), out_shape=(shape((3, dim,...  9.46 us
    all_to_all x1, starting transfers between devices, on_device(): lax.all_to_all(jnp.broadcast_to(proj_mine, (devices, owned, 3 * dim)), 'f...  9.36 us
    select_n x1, other arithmetic, on_device(): own_state = jnp.where(core == 0, state[0, 0], state[0, 1])  3.36 us
  transfers between devices with their start and end apart: 29, of which 7 were waited for; matrix products, arithmetic and copies ran while one was open for 9% of the time, Pallas kernels for 6%

profile of v1, /device:TPU:1, one launch (start us, length us, event | category | flops | bytes accessed | tf_op | source)
XLA Modules:
  0.0 159.3 jit_solution(11024408670184171220)
XLA Ops:
  2.8 9.4 %all-to-all-start = ((bf16[32,32,768]{2,1,0:T(8,128)(2,1)}), bf16[32,32,768]{2,1,0:T(8,128)(2,1)S(1)}, u32[]{:S(2)}, u32[]{:S(2)}) async-start(bf16[32,32,768]{2,1,0:T(8,128)(2,1)} %broadcast_in_dim.12), calls=%async_computation | async-start | bytes 3145728 | tf_op jit(solution)/shard_map/all_to_all | solution.py:253
  12.2 5.2 %collective-permute-start.16 = (f32[2,128]{1,0:T(2,128)S(1)}, f32[2,128]{1,0:T(2,128)S(1)}, u32[]{:S(2)}, u32[]{:S(2)}) collective-permute-start(f32[2,128]{1,0:T(2,128)S(1)} %bitcast.72), channel_id=1, source_target_pairs={{0,192},{32,224},{64,0},{96,32},{128,64},{160,96},{192,128},{224,1... | collective-permute-start | bytes 3080 | tf_op jit(solution)/shard_map/ppermute | solution.py:219
  18.6 2.1 %collective-permute-start.14 = (f32[2,128]{1,0:T(2,128)S(1)}, f32[2,128]{1,0:T(2,128)S(1)}, u32[]{:S(2)}, u32[]{:S(2)}) collective-permute-start(f32[2,128]{1,0:T(2,128)S(1)} %bitcast.74), channel_id=1, source_target_pairs={{0,64},{32,96},{64,128},{96,160},{128,192},{160,224},{192,0},{224,... | collective-permute-start | bytes 3080 | tf_op jit(solution)/shard_map/ppermute | solution.py:219
  22.3 4.2 %collective-permute-start.10 = (bf16[128,1024]{1,0:T(8,128)(2,1)S(1)}, bf16[128,1024]{1,0:T(8,128)(2,1)S(1)}, u32[]{:S(2)}, u32[]{:S(2)}) collective-permute-start(bf16[128,1024]{1,0:T(8,128)(2,1)S(1)} %get-tuple-element.29.refs_0_.refs_14_), channel_id=1, source_target_pairs={{0,128},{32,160},{64,192},{96,224},{128,0},{160,32},{192,64},{224,... | collective-permute-start | bytes 786440 | tf_op jit(solution)/shard_map/ppermute | solution.py:219
  26.5 3.4 %select_bitcast_fusion.refs_9_ = f32[3,256,512]{2,1,0:T(8,128)} fusion(f32[1,2,3,256,512]{4,3,2,1,0:T(8,128)} %param.7, pred[]{:T(512)S(6)} %eq.2), kind=kLoop, calls=%fused_computation.2 | loop fusion | flops 393216 | bytes 4718593 | tf_op jit(solution)/shard_map/jit(_where)/select_n | solution.py:256
  30.6 4.3 %collective-permute-done.15 = f32[2,128]{1,0:T(2,128)S(1)} collective-permute-done((f32[2,128]{1,0:T(2,128)S(1)}, f32[2,128]{1,0:T(2,128)S(1)}, u32[]{:S(2)}, u32[]{:S(2)}) %collective-permute-start.15) | collective-permute-done | bytes 1056 | tf_op jit(solution)/shard_map/ppermute | solution.py:219
  34.9 3.3 %collective-permute-start.4 = (bf16[2,128,256]{2,1,0:T(8,128)(2,1)S(1)}, bf16[2,128,256]{2,1,0:T(8,128)(2,1)S(1)}, u32[]{:S(2)}, u32[]{:S(2)}) collective-permute-start(bf16[2,128,256]{2,1,0:T(8,128)(2,1)S(1)} %get-tuple-element.34), channel_id=1, source_target_pairs={{0,32},{32,0},{64,96},{96,64},{128,160},{160,128},{192,224},{224,1... | collective-permute-start | bytes 393224 | tf_op jit(solution)/shard_map/ppermute | solution.py:214
  38.1 1.9 %collective-permute-start = (bf16[2,128,1024]{2,1,0:T(8,128)(2,1)S(1)}, bf16[2,128,1024]{2,1,0:T(8,128)(2,1)S(1)}, u32[]{:S(2)}, u32[]{:S(2)}) collective-permute-start(bf16[2,128,1024]{2,1,0:T(8,128)(2,1)S(1)} %bitcast.63), channel_id=1, source_target_pairs={{0,32},{32,0},{64,96},{96,64},{128,160},{160,128},{192,224},{224,1... | collective-permute-start | bytes 1572872 | tf_op jit(solution)/shard_map/ppermute | solution.py:214
  41.6 4.8 %collective-permute-start.7 = (bf16[256,256]{1,0:T(8,128)(2,1)S(1)}, bf16[256,256]{1,0:T(8,128)(2,1)}, u32[]{:S(2)}, u32[]{:S(2)}) collective-permute-start(bf16[256,256]{1,0:T(8,128)(2,1)S(1)} %pad_maximum_fusion.1.refs_4_), channel_id=1, source_target_pairs={{0,192},{32,224},{64,0},{96,32},{128,64},{160,96},{192,128},{224,1... | collective-permute-start | bytes 393224 | tf_op jit(solution)/shard_map/ppermute | solution.py:219
  46.5 2.8 %collective-permute-start.13 = (bf16[128,1024]{1,0:T(8,128)(2,1)S(1)}, bf16[128,1024]{1,0:T(8,128)(2,1)}, u32[]{:S(2)}, u32[]{:S(2)}) collective-permute-start(bf16[128,1024]{1,0:T(8,128)(2,1)S(1)} %collective-permute-done.12.refs_6_), channel_id=1, source_target_pairs={{0,32},{32,0},{64,96},{96,64},{128,160},{160,128},{192,224},{224,1... | collective-permute-start | bytes 786440 | tf_op jit(solution)/shard_map/ppermute | solution.py:214
  49.2 2.0 %collective-permute-done.8.refs_2_ = bf16[128,1024]{1,0:T(8,128)(2,1)S(1)} collective-permute-done((bf16[128,1024]{1,0:T(8,128)(2,1)S(1)}, bf16[128,1024]{1,0:T(8,128)(2,1)S(1)}, u32[]{:S(2)}, u32[]{:S(2)}) %collective-permute-start.8) | collective-permute-done | bytes 262176 | tf_op jit(solution)/shard_map/ppermute | solution.py:219
  54.0 6.9 %collective-permute-start.6 = (bf16[256,256]{1,0:T(8,128)(2,1)S(1)}, bf16[256,256]{1,0:T(8,128)(2,1)S(1)}, u32[]{:S(2)}, u32[]{:S(2)}) collective-permute-start(bf16[256,256]{1,0:T(8,128)(2,1)S(1)} %pad_maximum_fusion.1.refs_4_), channel_id=1, source_target_pairs={{0,128},{32,160},{64,192},{96,224},{128,0},{160,32},{192,64},{224,... | collective-permute-start | bytes 393224 | tf_op jit(solution)/shard_map/ppermute | solution.py:219
  60.9 1.9 %collective-permute-done.7.refs_7_ = bf16[256,256]{1,0:T(8,128)(2,1)} collective-permute-done((bf16[256,256]{1,0:T(8,128)(2,1)S(1)}, bf16[256,256]{1,0:T(8,128)(2,1)}, u32[]{:S(2)}, u32[]{:S(2)}) %collective-permute-start.7) | collective-permute-done | bytes 131104 | tf_op jit(solution)/shard_map/ppermute | solution.py:219
  62.7 2.4 %collective-permute-start.5 = (bf16[256,256]{1,0:T(8,128)(2,1)S(1)}, bf16[256,256]{1,0:T(8,128)(2,1)S(1)}, u32[]{:S(2)}, u32[]{:S(2)}) collective-permute-start(bf16[256,256]{1,0:T(8,128)(2,1)S(1)} %pad_maximum_fusion.1.refs_4_), channel_id=1, source_target_pairs={{0,64},{32,96},{64,128},{96,160},{128,192},{160,224},{192,0},{224,... | collective-permute-start | bytes 393224 | tf_op jit(solution)/shard_map/ppermute | solution.py:219
  66.3 2.4 %collective-permute-start.2 = (bf16[256,256]{1,0:T(8,128)(2,1)S(1)}, bf16[256,256]{1,0:T(8,128)(2,1)S(1)}, u32[]{:S(2)}, u32[]{:S(2)}) collective-permute-start(bf16[256,256]{1,0:T(8,128)(2,1)S(1)} %convolution_convert_fusion.refs_0_), channel_id=1, source_target_pairs={{0,128},{32,160},{64,192},{96,224},{128,0},{160,32},{192,64},{224,... | collective-permute-start | bytes 393224 | tf_op jit(solution)/shard_map/ppermute | solution.py:219
  69.4 9.5 %update.1 = (bf16[3,256,512]{2,1,0:T(8,128)(2,1)}, bf16[256,512]{1,0:T(8,128)(2,1)}, f32[3,256,512]{2,1,0:T(8,128)}, bf16[256,256]{1,0:T(8,128)(2,1)}) custom-call(bf16[128,1024]{1,0:T(8,128)(2,1)} %copy-done.4, bf16[128,1024]{1,0:T(8,128)(2,1)} %get-tuple-element.27.refs_1_.refs_15_, bf16[128,1024]{1,0:T(8,128)(2,1)} %copy-done.14, ...), custom_call_target="tpu_custom_call" | custom-call | tf_op jit(solution)/shard_map/update/pallas_call | solution.py:264
  81.1 10.5 %late.1 = (f32[3,64,512]{2,1,0:T(8,128)}, bf16[4,3,64,512]{3,2,1,0:T(8,128)(2,1)}, bf16[1024,768]{1,0:T(8,128)(2,1)}, bf16[256,768]{1,0:T(8,128)(2,1)}, bf16[256,256]{1,0:T(8,128)(2,1)}) custom-call(s32[1]{0:T(128)} %bitcast.place, bf16[256,256]{1,0:T(8,128)(2,1)} %copy-done.17, bf16[256,256]{1,0:T(8,128)(2,1)} %copy-done.22, bf16[256,256]{1,0:T(8,128)(2,1)} %copy-done.21, ...), custom_call_target="tpu_custom_call" | custom-call | tf_op jit(solution)/shard_map/late/pallas_call | solution.py:284
  91.6 12.6 %all-to-all-start.1 = ((bf16[32,32,768]{2,1,0:T(8,128)(2,1)}), bf16[32,32,768]{2,1,0:T(8,128)(2,1)}, u32[]{:S(2)}, u32[]{:S(2)}) async-start(bf16[32,32,768]{2,1,0:T(8,128)(2,1)} %bitcast.62), calls=%async_computation.1 | async-start | bytes 3145728 | tf_op jit(solution)/shard_map/all_to_all | solution.py:319
  104.4 2.2 %collective-permute-start.19 = (bf16[3,64,512]{2,1,0:T(8,128)(2,1)S(1)}, bf16[3,64,512]{2,1,0:T(8,128)(2,1)S(1)}, u32[]{:S(2)}, u32[]{:S(2)}) collective-permute-start(bf16[3,64,512]{2,1,0:T(8,128)(2,1)S(1)} %get-tuple-element.24), channel_id=1, source_target_pairs={{0,64},{32,96},{64,128},{96,160},{128,192},{160,224},{192,0},{224,... | collective-permute-start | bytes 589832 | tf_op jit(solution)/shard_map/ppermute | solution.py:219
  108.0 5.0 %collective-permute-start.20 = (bf16[3,64,512]{2,1,0:T(8,128)(2,1)S(1)}, bf16[3,64,512]{2,1,0:T(8,128)(2,1)S(1)}, u32[]{:S(2)}, u32[]{:S(2)}) collective-permute-start(bf16[3,64,512]{2,1,0:T(8,128)(2,1)S(1)} %get-tuple-element.26), channel_id=1, source_target_pairs={{0,128},{32,160},{64,192},{96,224},{128,0},{160,32},{192,64},{224,... | collective-permute-start | bytes 589832 | tf_op jit(solution)/shard_map/ppermute | solution.py:219
  114.0 18.4 %collective-permute-done.19 = bf16[3,64,512]{2,1,0:T(8,128)(2,1)S(1)} collective-permute-done((bf16[3,64,512]{2,1,0:T(8,128)(2,1)S(1)}, bf16[3,64,512]{2,1,0:T(8,128)(2,1)S(1)}, u32[]{:S(2)}, u32[]{:S(2)}) %collective-permute-start.19) | collective-permute-done | bytes 196640 | tf_op jit(solution)/shard_map/ppermute | solution.py:219
  132.4 9.4 %collective-permute-done.20 = bf16[3,64,512]{2,1,0:T(8,128)(2,1)S(1)} collective-permute-done((bf16[3,64,512]{2,1,0:T(8,128)(2,1)S(1)}, bf16[3,64,512]{2,1,0:T(8,128)(2,1)S(1)}, u32[]{:S(2)}, u32[]{:S(2)}) %collective-permute-start.20) | collective-permute-done | bytes 196640 | tf_op jit(solution)/shard_map/ppermute | solution.py:219
  151.8 3.6 %collective-permute-done.24 = bf16[32,768]{1,0:T(8,128)(2,1)S(1)} collective-permute-done((bf16[32,768]{1,0:T(8,128)(2,1)S(1)}, bf16[32,768]{1,0:T(8,128)(2,1)S(1)}, u32[]{:S(2)}, u32[]{:S(2)}) %collective-permute-start.24) | collective-permute-done | bytes 49184 | tf_op jit(solution)/shard_map/ppermute | solution.py:219
  155.3 2.0 %collective-permute-start.26 = (f32[32,768]{1,0:T(8,128)S(1)}, f32[32,768]{1,0:T(8,128)S(1)}, u32[]{:S(2)}, u32[]{:S(2)}) collective-permute-start(f32[32,768]{1,0:T(8,128)S(1)} %convert_add_fusion.1), channel_id=1, source_target_pairs={{0,32},{32,0},{64,96},{96,64},{128,160},{160,128},{192,224},{224,1... | collective-permute-start | bytes 294920 | tf_op jit(solution)/shard_map/ppermute | solution.py:214
  (116 shorter events, 28.1 us)
Async XLA Ops:
  2.8 50.8 %all-to-all-start = ((bf16[32,32,768]{2,1,0:T(8,128)(2,1)}), bf16[32,32,768]{2,1,0:T(8,128)(2,1)S(1)}, u32[]{:S(2)}, u32[]{:S(2)}) async-start(bf16[32,32,768]{2,1,0:T(8,128)(2,1)} %broadcast_in_dim.12), calls=%async_computation | async-start | bytes 3145728 | tf_op jit(solution)/shard_map/all_to_all | solution.py:253
  12.2 18.3 %collective-permute-start.16 = (f32[2,128]{1,0:T(2,128)S(1)}, f32[2,128]{1,0:T(2,128)S(1)}, u32[]{:S(2)}, u32[]{:S(2)}) collective-permute-start(f32[2,128]{1,0:T(2,128)S(1)} %bitcast.72), channel_id=1, source_target_pairs={{0,192},{32,224},{64,0},{96,32},{128,64},{160,96},{192,128},{224,1... | collective-permute-start | bytes 3080 | tf_op jit(solution)/shard_map/ppermute | solution.py:219
  17.4 17.5 %collective-permute-start.15 = (f32[2,128]{1,0:T(2,128)S(1)}, f32[2,128]{1,0:T(2,128)S(1)}, u32[]{:S(2)}, u32[]{:S(2)}) collective-permute-start(f32[2,128]{1,0:T(2,128)S(1)} %bitcast.73), channel_id=1, source_target_pairs={{0,128},{32,160},{64,192},{96,224},{128,0},{160,32},{192,64},{224,... | collective-permute-start | bytes 3080 | tf_op jit(solution)/shard_map/ppermute | solution.py:219
  18.6 19.5 %collective-permute-start.14 = (f32[2,128]{1,0:T(2,128)S(1)}, f32[2,128]{1,0:T(2,128)S(1)}, u32[]{:S(2)}, u32[]{:S(2)}) collective-permute-start(f32[2,128]{1,0:T(2,128)S(1)} %bitcast.74), channel_id=1, source_target_pairs={{0,64},{32,96},{64,128},{96,160},{128,192},{160,224},{192,0},{224,... | collective-permute-start | bytes 3080 | tf_op jit(solution)/shard_map/ppermute | solution.py:219
  20.7 20.9 %collective-permute-start.12 = (bf16[128,1024]{1,0:T(8,128)(2,1)S(1)}, bf16[128,1024]{1,0:T(8,128)(2,1)S(1)}, u32[]{:S(2)}, u32[]{:S(2)}) collective-permute-start(bf16[128,1024]{1,0:T(8,128)(2,1)S(1)} %get-tuple-element.29.refs_0_.refs_14_), channel_id=1, source_target_pairs={{0,192},{32,224},{64,0},{96,32},{128,64},{160,96},{192,128},{224,1... | collective-permute-start | bytes 786440 | tf_op jit(solution)/shard_map/ppermute | solution.py:219
  22.3 24.2 %collective-permute-start.10 = (bf16[128,1024]{1,0:T(8,128)(2,1)S(1)}, bf16[128,1024]{1,0:T(8,128)(2,1)S(1)}, u32[]{:S(2)}, u32[]{:S(2)}) collective-permute-start(bf16[128,1024]{1,0:T(8,128)(2,1)S(1)} %get-tuple-element.29.refs_0_.refs_14_), channel_id=1, source_target_pairs={{0,128},{32,160},{64,192},{96,224},{128,0},{160,32},{192,64},{224,... | collective-permute-start | bytes 786440 | tf_op jit(solution)/shard_map/ppermute | solution.py:219
  30.6 20.7 %collective-permute-start.8 = (bf16[128,1024]{1,0:T(8,128)(2,1)S(1)}, bf16[128,1024]{1,0:T(8,128)(2,1)S(1)}, u32[]{:S(2)}, u32[]{:S(2)}) collective-permute-start(bf16[128,1024]{1,0:T(8,128)(2,1)S(1)} %get-tuple-element.29.refs_0_.refs_14_), channel_id=1, source_target_pairs={{0,64},{32,96},{64,128},{96,160},{128,192},{160,224},{192,0},{224,... | collective-permute-start | bytes 786440 | tf_op jit(solution)/shard_map/ppermute | solution.py:219
  38.1 14.7 %collective-permute-start = (bf16[2,128,1024]{2,1,0:T(8,128)(2,1)S(1)}, bf16[2,128,1024]{2,1,0:T(8,128)(2,1)S(1)}, u32[]{:S(2)}, u32[]{:S(2)}) collective-permute-start(bf16[2,128,1024]{2,1,0:T(8,128)(2,1)S(1)} %bitcast.63), channel_id=1, source_target_pairs={{0,32},{32,0},{64,96},{96,64},{128,160},{160,128},{192,224},{224,1... | collective-permute-start | bytes 1572872 | tf_op jit(solution)/shard_map/ppermute | solution.py:214
  40.0 14.0 %collective-permute-start.17 = (f32[4,128]{1,0:T(4,128)S(1)}, f32[4,128]{1,0:T(4,128)S(1)}, u32[]{:S(2)}, u32[]{:S(2)}) collective-permute-start(f32[4,128]{1,0:T(4,128)S(1)} %bitcast.71), channel_id=1, source_target_pairs={{0,32},{32,0},{64,96},{96,64},{128,160},{160,128},{192,224},{224,1... | collective-permute-start | bytes 6152 | tf_op jit(solution)/shard_map/ppermute | solution.py:214
  41.6 21.1 %collective-permute-start.7 = (bf16[256,256]{1,0:T(8,128)(2,1)S(1)}, bf16[256,256]{1,0:T(8,128)(2,1)}, u32[]{:S(2)}, u32[]{:S(2)}) collective-permute-start(bf16[256,256]{1,0:T(8,128)(2,1)S(1)} %pad_maximum_fusion.1.refs_4_), channel_id=1, source_target_pairs={{0,192},{32,224},{64,0},{96,32},{128,64},{160,96},{192,128},{224,1... | collective-permute-start | bytes 393224 | tf_op jit(solution)/shard_map/ppermute | solution.py:219
  46.5 18.7 %collective-permute-start.13 = (bf16[128,1024]{1,0:T(8,128)(2,1)S(1)}, bf16[128,1024]{1,0:T(8,128)(2,1)}, u32[]{:S(2)}, u32[]{:S(2)}) collective-permute-start(bf16[128,1024]{1,0:T(8,128)(2,1)S(1)} %collective-permute-done.12.refs_6_), channel_id=1, source_target_pairs={{0,32},{32,0},{64,96},{96,64},{128,160},{160,128},{192,224},{224,1... | collective-permute-start | bytes 786440 | tf_op jit(solution)/shard_map/ppermute | solution.py:214
  51.3 15.0 %collective-permute-start.11 = (bf16[128,1024]{1,0:T(8,128)(2,1)S(1)}, bf16[128,1024]{1,0:T(8,128)(2,1)}, u32[]{:S(2)}, u32[]{:S(2)}) collective-permute-start(bf16[128,1024]{1,0:T(8,128)(2,1)S(1)} %collective-permute-done.10.refs_4_), channel_id=1, source_target_pairs={{0,32},{32,0},{64,96},{96,64},{128,160},{160,128},{192,224},{224,1... | collective-permute-start | bytes 786440 | tf_op jit(solution)/shard_map/ppermute | solution.py:214
  52.8 15.9 %collective-permute-start.9 = (bf16[128,1024]{1,0:T(8,128)(2,1)S(1)}, bf16[128,1024]{1,0:T(8,128)(2,1)S(1)}, u32[]{:S(2)}, u32[]{:S(2)}) collective-permute-start(bf16[128,1024]{1,0:T(8,128)(2,1)S(1)} %collective-permute-done.8.refs_2_), channel_id=1, source_target_pairs={{0,32},{32,0},{64,96},{96,64},{128,160},{160,128},{192,224},{224,1... | collective-permute-start | bytes 786440 | tf_op jit(solution)/shard_map/ppermute | solution.py:214
  54.0 24.9 %collective-permute-start.6 = (bf16[256,256]{1,0:T(8,128)(2,1)S(1)}, bf16[256,256]{1,0:T(8,128)(2,1)S(1)}, u32[]{:S(2)}, u32[]{:S(2)}) collective-permute-start(bf16[256,256]{1,0:T(8,128)(2,1)S(1)} %pad_maximum_fusion.1.refs_4_), channel_id=1, source_target_pairs={{0,128},{32,160},{64,192},{96,224},{128,0},{160,32},{192,64},{224,... | collective-permute-start | bytes 393224 | tf_op jit(solution)/shard_map/ppermute | solution.py:219
  62.7 16.2 %collective-permute-start.5 = (bf16[256,256]{1,0:T(8,128)(2,1)S(1)}, bf16[256,256]{1,0:T(8,128)(2,1)S(1)}, u32[]{:S(2)}, u32[]{:S(2)}) collective-permute-start(bf16[256,256]{1,0:T(8,128)(2,1)S(1)} %pad_maximum_fusion.1.refs_4_), channel_id=1, source_target_pairs={{0,64},{32,96},{64,128},{96,160},{128,192},{160,224},{192,0},{224,... | collective-permute-start | bytes 393224 | tf_op jit(solution)/shard_map/ppermute | solution.py:219
  65.1 13.8 %collective-permute-start.3 = (bf16[256,256]{1,0:T(8,128)(2,1)S(1)}, bf16[256,256]{1,0:T(8,128)(2,1)S(1)}, u32[]{:S(2)}, u32[]{:S(2)}) collective-permute-start(bf16[256,256]{1,0:T(8,128)(2,1)S(1)} %convolution_convert_fusion.refs_0_), channel_id=1, source_target_pairs={{0,192},{32,224},{64,0},{96,32},{128,64},{160,96},{192,128},{224,1... | collective-permute-start | bytes 393224 | tf_op jit(solution)/shard_map/ppermute | solution.py:219
  66.3 12.7 %collective-permute-start.2 = (bf16[256,256]{1,0:T(8,128)(2,1)S(1)}, bf16[256,256]{1,0:T(8,128)(2,1)S(1)}, u32[]{:S(2)}, u32[]{:S(2)}) collective-permute-start(bf16[256,256]{1,0:T(8,128)(2,1)S(1)} %convolution_convert_fusion.refs_0_), channel_id=1, source_target_pairs={{0,128},{32,160},{64,192},{96,224},{128,0},{160,32},{192,64},{224,... | collective-permute-start | bytes 393224 | tf_op jit(solution)/shard_map/ppermute | solution.py:219
  68.7 11.7 %collective-permute-start.1 = (bf16[256,256]{1,0:T(8,128)(2,1)S(1)}, bf16[256,256]{1,0:T(8,128)(2,1)S(1)}, u32[]{:S(2)}, u32[]{:S(2)}) collective-permute-start(bf16[256,256]{1,0:T(8,128)(2,1)S(1)} %convolution_convert_fusion.refs_0_), channel_id=1, source_target_pairs={{0,64},{32,96},{64,128},{96,160},{128,192},{160,224},{192,0},{224,... | collective-permute-start | bytes 393224 | tf_op jit(solution)/shard_map/ppermute | solution.py:219
  91.6 52.9 %all-to-all-start.1 = ((bf16[32,32,768]{2,1,0:T(8,128)(2,1)}), bf16[32,32,768]{2,1,0:T(8,128)(2,1)}, u32[]{:S(2)}, u32[]{:S(2)}) async-start(bf16[32,32,768]{2,1,0:T(8,128)(2,1)} %bitcast.62), calls=%async_computation.1 | async-start | bytes 3145728 | tf_op jit(solution)/shard_map/all_to_all | solution.py:319
  104.4 28.0 %collective-permute-start.19 = (bf16[3,64,512]{2,1,0:T(8,128)(2,1)S(1)}, bf16[3,64,512]{2,1,0:T(8,128)(2,1)S(1)}, u32[]{:S(2)}, u32[]{:S(2)}) collective-permute-start(bf16[3,64,512]{2,1,0:T(8,128)(2,1)S(1)} %get-tuple-element.24), channel_id=1, source_target_pairs={{0,64},{32,96},{64,128},{96,160},{128,192},{160,224},{192,0},{224,... | collective-permute-start | bytes 589832 | tf_op jit(solution)/shard_map/ppermute | solution.py:219
  106.6 25.8 %collective-permute-start.21 = (bf16[3,64,512]{2,1,0:T(8,128)(2,1)S(1)}, bf16[3,64,512]{2,1,0:T(8,128)(2,1)S(1)}, u32[]{:S(2)}, u32[]{:S(2)}) collective-permute-start(bf16[3,64,512]{2,1,0:T(8,128)(2,1)S(1)} %get-tuple-element.25), channel_id=1, source_target_pairs={{0,192},{32,224},{64,0},{96,32},{128,64},{160,96},{192,128},{224,1... | collective-permute-start | bytes 589832 | tf_op jit(solution)/shard_map/ppermute | solution.py:219
  108.0 33.8 %collective-permute-start.20 = (bf16[3,64,512]{2,1,0:T(8,128)(2,1)S(1)}, bf16[3,64,512]{2,1,0:T(8,128)(2,1)S(1)}, u32[]{:S(2)}, u32[]{:S(2)}) collective-permute-start(bf16[3,64,512]{2,1,0:T(8,128)(2,1)S(1)} %get-tuple-element.26), channel_id=1, source_target_pairs={{0,128},{32,160},{64,192},{96,224},{128,0},{160,32},{192,64},{224,... | collective-permute-start | bytes 589832 | tf_op jit(solution)/shard_map/ppermute | solution.py:219
  144.4 13.0 %collective-permute-start.18 = (bf16[2,128,1024]{2,1,0:T(8,128)(2,1)S(1)}, bf16[2,128,1024]{2,1,0:T(8,128)(2,1)S(1)}, u32[]{:S(2)}, u32[]{:S(2)}) collective-permute-start(bf16[2,128,1024]{2,1,0:T(8,128)(2,1)S(1)} %fusion.3), channel_id=1, source_target_pairs={{0,32},{32,0},{64,96},{96,64},{128,160},{160,128},{192,224},{224,1... | collective-permute-start | bytes 1572872 | tf_op jit(solution)/shard_map/ppermute | solution.py:214
  147.8 7.6 %collective-permute-start.24 = (bf16[32,768]{1,0:T(8,128)(2,1)S(1)}, bf16[32,768]{1,0:T(8,128)(2,1)S(1)}, u32[]{:S(2)}, u32[]{:S(2)}) collective-permute-start(bf16[32,768]{1,0:T(8,128)(2,1)S(1)} %reduce_sum.12), channel_id=1, source_target_pairs={{0,128},{32,160},{64,192},{96,224},{128,0},{160,32},{192,64},{224,... | collective-permute-start | bytes 147464 | tf_op jit(solution)/shard_map/ppermute | solution.py:219
  (30 other events, 439.1 us)

commit v2 on v1

--- a/solution.py
+++ b/solution.py
@@ -59,42 +59,69 @@
     return d_gate, d_up, hidden
 
 
-def update_kernel(count, *refs):
-    tok = refs[: 2 * count]
-    proj, state, rates, cot0, cot0_mate = refs[2 * count : 2 * count + 5]
-    next_ref, kv_ref, early_ref, dq_ref = refs[2 * count + 5 : 2 * count + 9]
-    keys, w16, total = refs[2 * count + 9 :]
-    rows = tok[0].shape[0]
+def piece_refs(refs, count):
+    pieces = []
+    for ref in refs[: 2 * (count - 1)]:
+        half = ref.shape[1] // 2
+        pieces.append((ref.at[:, :half], ref.at[:, half:]))
+    for low, high in zip(refs[2 * (count - 1) :: 2], refs[2 * (count - 1) + 1 :: 2]):
+        pieces.append((low, high))
+    return pieces
+
+
+def piece_rate(piece, rows, head):
+    low, width = piece[0], rows
+    row = rows
+    line = low[row : row + 16, :].astype(F32)
+    halves = []
+    for level in range(2):
+        pick = line[0:1, level * CORES * width : (level * CORES + 1) * width]
+        rest = line[0:1, (level * CORES + 1) * width : (level + 1) * CORES * width]
+        halves.append(jnp.where(head == 0, pick, rest))
+    return as_column(halves[0] + halves[1])
+
+
+def early_kernel(whole, state, tok, tok_mate, cot, cot_mate, early_ref, dq_ref):
     dim = state.shape[1]
-    span = 2 * rows
-    for part in range(3):
-        w16[part] = state[part].astype(BF)
-    weights = (w16[0], w16[1], w16[2])
-    own = jnp.concatenate([tok[0][...], tok[1][...]], axis=0)
-    query = dot_nn(own, proj[:, :dim]).astype(BF).astype(F32)
+    w1, w3, w2 = (state[part].astype(BF) for part in range(3))
+    own = jnp.concatenate([tok[...], tok_mate[...]], axis=0)
+    query = dot_nn(own, whole[:, :dim]).astype(BF).astype(F32)
     scale = inverse_rms(query)
     unit = query * scale
     unit16 = unit.astype(BF)
-    cot = jnp.concatenate([cot0[...], cot0_mate[...]], axis=0)
-    d_gate, d_up, hidden = weight_terms(unit16, cot, weights)
+    cots = jnp.concatenate([cot[...], cot_mate[...]], axis=0)
+    d_gate, d_up, hidden = weight_terms(unit16, cots, (w1, w3, w2))
     early_ref[0] = dot_tn(unit16, d_gate)
     early_ref[1] = dot_tn(unit16, d_up)
-    early_ref[2] = dot_tn(cot, hidden)
-    pulled = dot_nt(d_gate, weights[0]) + dot_nt(d_up, weights[1])
+    early_ref[2] = dot_tn(cots, hidden)
+    pulled = dot_nt(d_gate, w1) + dot_nt(d_up, w3)
     dq_ref[...] = unit_pull(pulled, unit, scale).astype(BF)
 
-    for block in range(count):
-        both = jnp.concatenate([tok[2 * block][...], tok[2 * block + 1][...]], axis=0)
-        keys[pl.ds(block * span, span), :] = dot_nn(both, proj[:, dim:]).astype(BF)
-    kv_ref[...] = keys[pl.ds(0, span), :]
+
+def update_kernel(count, rows, head_ref, *refs):
+    refs = list(refs)
+    pieces = piece_refs(refs[: 2 * count + 2], count)
+    whole, state, next_ref, kv_ref, rate_ref, keys, w16, total = refs[2 * count + 2 :]
+    dim = state.shape[1]
+    half = whole.shape[0] // 2
+    head = head_ref[0]
     for part in range(3):
+        w16[part] = state[part].astype(BF)
         total[part] = state[part]
+    for index, piece in enumerate(pieces):
+        out = dot_nn(piece[0][:rows, :], whole[:half, dim:])
+        out = out + dot_nn(piece[1][:rows, :], whole[half:, dim:])
+        keys[index * rows : (index + 1) * rows, :] = out.astype(BF)
+        rate_ref[index * rows : (index + 1) * rows, :] = jnp.broadcast_to(
+            piece_rate(piece, rows, head), (rows, rate_ref.shape[1])
+        )
+    span = CORES * rows
+    kv_ref[...] = keys[:span, :]
 
     def step(block, carry):
-        pair = keys[pl.ds(pl.multiple_of(block * span, span), span), :].astype(F32)
-        rate = jnp.concatenate(
-            [as_column(rates[pl.ds(2 * block + half, 1), :]) for half in range(2)], axis=0
-        )
+        at = pl.ds(pl.multiple_of(block * span, span), span)
+        pair = keys[at, :].astype(F32)
+        rate = rate_ref[at, :1]
         key = pair[:, :dim]
         unit16 = (key * inverse_rms(key)).astype(BF)
         cot = (pair[:, dim:] * rate).astype(BF)
@@ -109,14 +136,16 @@
         next_ref[part] = total[part].astype(BF)
 
 
-def late_kernel(count, place, *refs):
-    queries = refs[:count]
-    cots = refs[count : 2 * count]
+def late_kernel(count, rows, place, *refs):
+    refs = list(refs)
+    dim = refs[count + 2].shape[1]
+    queries = [ref.at[:, :dim] for ref in refs[: count - 1]] + [refs[count - 1]]
+    cots = [ref.at[:, dim:] for ref in refs[: count - 1]] + [refs[count]]
     (next_w, state, rates, kv, early, dq0, tok0, tok0_mate, tok1, tok1_mate) = refs[
-        2 * count : 2 * count + 10
+        count + 1 : count + 11
     ]
-    (own_ref, share_ref, dproj_ref, g0_ref, g1_ref) = refs[2 * count + 10 : 2 * count + 15]
-    w16, c16, units, total = refs[2 * count + 15 :]
+    (own_ref, share_ref, dproj_ref, g0_ref, g1_ref) = refs[count + 11 : count + 16]
+    w16, c16, total = refs[count + 16 :]
     span, dim = kv.shape[0], state.shape[1]
     share = dim // count
     for part in range(3):
@@ -144,7 +173,7 @@
 
     pair = kv[...].astype(F32)
     key, value = pair[:, :dim], pair[:, dim:]
-    rate = jnp.concatenate([as_column(rates[half : half + 1, :]) for half in range(2)], axis=0)
+    rate = rates[:span, :1]
     scale = inverse_rms(key)
     unit = key * scale
     unit16 = unit.astype(BF)
@@ -185,7 +214,7 @@
 
     def project(step, carry):
         at = pl.ds(pl.multiple_of(step * columns, columns), columns)
-        first = jnp.concatenate([tok0[:, at], tok0_mate[:, at]], axis=0)
+        first = jnp.concatenate([tok0[:rows, at], tok0_mate[:rows, at]], axis=0)
         second = jnp.concatenate([tok1[:, at], tok1_mate[:, at]], axis=0)
         out = dot_tn(first, g0_ref[...])
         extra = dot_tn(second, g1_ref[...])
@@ -223,66 +252,102 @@
         )
 
     hops = range(1, groups)
+    flat = lax.axis_index("fsdp")
+    side = lax.rem(flat, 2)
+    devices = lax.axis_size("fsdp")
+    planes = [list(range(first, devices, 2)) for first in range(2)]
+    plane = devices // 2
+
+    def across(value):
+        return lax.ppermute(value, "fsdp", [(i, i + 1 - 2 * (i % 2)) for i in range(devices)])
 
     def mine(value):
         half = value.shape[-1] // CORES
         return jnp.where(core == 0, value[..., :half], value[..., half:])
 
-    def other(value):
-        half = value.shape[-1] // CORES
-        return jnp.where(core == 0, value[..., half:], value[..., :half])
+    proj_mine = mine(proj).reshape(owned, 3 * dim)
+    proj_pair = across(proj_mine)
+    both = jnp.where(
+        side == 0,
+        jnp.concatenate([proj_mine, proj_pair], axis=0),
+        jnp.concatenate([proj_pair, proj_mine], axis=0),
+    )
+    own_state = jnp.where(core == 0, state[0, 0], state[0, 1])
 
     tok = tokens[0]
-    tok_mate = to_mate(tok)
-    pieces = [tok[0], tok_mate[0]]
-    far = [along(tok[0], hop) for hop in hops]
-    for item in far:
-        pieces += [item, to_mate(item)]
+    half_rows = rows // 2
+    rate_high = step_rates[0].astype(BF)
+    rate_low = (step_rates[0] - rate_high.astype(F32)).astype(BF)
+    rate_line = jnp.concatenate([rate_high[0], rate_high[1], rate_low[0], rate_low[1]])
+    rate_rows = jnp.broadcast_to(jnp.tile(rate_line, width // (4 * rows)), (16, width))
+    packed = jnp.concatenate([tok[0], rate_rows], axis=0)
+    local_mate = to_mate(jnp.concatenate([packed, tok[1]], axis=0))
+    both, local_mate = lax.optimization_barrier((both, local_mate))
+    whole = lax.all_to_all(
+        jnp.broadcast_to(both, (plane, 2 * owned, 3 * dim)),
+        "fsdp",
+        0,
+        0,
+        axis_index_groups=planes,
+        tiled=True,
+    ).reshape(devices * owned, 3 * dim)
+    packed_mate = local_mate[: packed.shape[0]]
+    tok1_mate = local_mate[packed.shape[0] :]
+    head_dim = d_out.shape[-1] // CORES
     cot = mine(d_out[0])
-    cot_mate = to_mate(other(d_out[0]))
-    cot1 = jnp.concatenate([cot[1], cot_mate[1]], axis=0)
-    cots = [cot1] + [along(cot1, hop) for hop in hops]
-    rate = step_rates[0]
-    all_rates = jnp.stack([rate] + [along(rate, hop) for hop in hops])
-    rate_mine = jnp.where(core == 0, all_rates[:, 0], all_rates[:, 1])
-    rate_mate = to_mate(jnp.where(core == 0, all_rates[:, 1], all_rates[:, 0]))
-    rates = jnp.stack([rate_mine, rate_mate], axis=1).reshape(groups * CORES, rows)
-
-    proj_mine = mine(proj).reshape(1, owned, 3 * dim)
-    devices = lax.axis_size("fsdp")
-    whole = lax.all_to_all(
-        jnp.broadcast_to(proj_mine, (devices, owned, 3 * dim)), "fsdp", 0, 0, tiled=True
-    ).reshape(devices * owned, 3 * dim)
-    own_state = jnp.where(core == 0, state[0, 0], state[0, 1])
-
-    second = jnp.concatenate([tok[1], tok_mate[1]], axis=0)
+    cot_mate = to_mate(jnp.where(core == 0, d_out[0, :, :, head_dim:], d_out[0, :, :, :head_dim]))
+    cot0, cot0_mate = cot[0], cot_mate[0]
+    ahead = along(packed, 1)
+    behind = along(packed, groups - 1)
+    far_low = along(ahead[:, : width // 2], 1)
+    far_high = along(behind[:, width // 2 :], groups - 1)
+    pieces = [packed, packed_mate, ahead, to_mate(ahead), behind, to_mate(behind)]
+    pieces += [far_low, far_high, to_mate(far_low), to_mate(far_high)]
+
+    second = jnp.concatenate([tok[1], tok1_mate], axis=0)
     query1 = jnp.dot(second, whole[:, :dim], preferred_element_type=F32).astype(BF)
-    queries = [query1] + [along(query1, hop) for hop in hops]
+    late_in = jnp.concatenate([query1, jnp.concatenate([cot[1], cot_mate[1]], axis=0)], axis=1)
+    late_in, far_low, far_high = lax.optimization_barrier((late_in, far_low, far_high))
+    late_ahead = along(late_in, 1)
+    late_behind = along(late_in, groups - 1)
+    lates = [late_in, late_ahead, late_behind]
+    lates += [along(late_ahead[:, :dim], 1), along(late_behind[:, dim:], groups - 1)]
 
     shape = jax.ShapeDtypeStruct
     params = pltpu.CompilerParams(vmem_limit_bytes=56 * 2**20)
-    next16, kv, early, dq0 = pl.pallas_call(
-        partial(update_kernel, groups),
+    early, dq0 = pl.pallas_call(
+        early_kernel,
+        out_shape=(shape((3, dim, hid), F32), shape((span, dim), BF)),
+        in_specs=[VMEM] * 6,
+        out_specs=(VMEM,) * 2,
+        compiler_params=params,
+        cost_estimate=pl.CostEstimate(flops=4*10**9, bytes_accessed=6 * 2**20, transcendentals=0),
+        name="early",
+    )(whole, own_state, tok[0], packed_mate[:rows], cot0, cot0_mate)
+
+    spots = jnp.stack([place, core]).astype(jnp.int32)
+    next16, kv, rates = pl.pallas_call(
+        partial(update_kernel, groups, rows),
         out_shape=(
             shape((3, dim, hid), BF),
             shape((span, 2 * dim), BF),
-            shape((3, dim, hid), F32),
-            shape((span, dim), BF),
+            shape((groups * span, 128), F32),
         ),
-        in_specs=[VMEM] * (2 * groups + 5),
-        out_specs=(VMEM,) * 4,
+        in_specs=[SMEM] + [VMEM] * (2 * groups + 4),
+        out_specs=(VMEM,) * 3,
         scratch_shapes=[
             pltpu.VMEM((groups * span, 2 * dim), BF),
             pltpu.VMEM((3, dim, hid), BF),
             pltpu.VMEM((3, dim, hid), F32),
         ],
         compiler_params=params,
+        cost_estimate=pl.CostEstimate(flops=9*10**9, bytes_accessed=6 * 2**20, transcendentals=0),
         name="update",
-    )(*pieces, whole, own_state, rates, cot[0], cot_mate[0])
+    )(core.reshape(1).astype(jnp.int32), *pieces, whole, own_state)
 
     share = dim // groups
     carried, shares, dproj, grads0, grads1 = pl.pallas_call(
-        partial(late_kernel, groups),
+        partial(late_kernel, groups, rows),
         out_shape=(
             shape((3, share, hid), F32),
             shape((groups, 3, share, hid), BF),
@@ -290,34 +355,43 @@
             shape((span, 3 * dim), BF),
             shape((span, dim), BF),
         ),
-        in_specs=[SMEM] + [VMEM] * (2 * groups + 10),
+        in_specs=[SMEM] + [VMEM] * (groups + 11),
         out_specs=(VMEM,) * 5,
         scratch_shapes=[
             pltpu.VMEM((3, dim, hid), BF),
             pltpu.VMEM((3, dim, hid), BF),
-            pltpu.VMEM((8, 128), F32),
             pltpu.VMEM((3, dim, hid), F32),
         ],
         compiler_params=params,
+        cost_estimate=pl.CostEstimate(flops=11*10**9, bytes_accessed=6 * 2**20, transcendentals=0),
         name="late",
     )(
-        place.reshape(1).astype(jnp.int32),
-        *queries,
-        *cots,
+        spots,
+        *lates,
         next16,
         own_state,
         rates,
         kv,
         early,
         dq0,
-        tok[0],
-        tok_mate[0],
+        packed,
+        packed_mate,
         tok[1],
-        tok_mate[1],
-    )
-
-    swapped = lax.all_to_all(dproj.reshape(devices, owned, 3 * dim), "fsdp", 0, 0, tiled=True)
-    owner = jnp.sum(swapped.astype(F32), axis=0).astype(BF)
+        tok1_mate,
+    )
+
+    swapped = lax.all_to_all(
+        dproj.reshape(plane, 2 * owned, 3 * dim),
+        "fsdp",
+        0,
+        0,
+        axis_index_groups=planes,
+        tiled=True,
+    )
+    pair_sum = jnp.sum(swapped.astype(F32), axis=0)
+    pair_keep = jnp.where(side == 0, pair_sum[:owned], pair_sum[owned:])
+    pair_give = jnp.where(side == 0, pair_sum[owned:], pair_sum[:owned]).astype(BF)
+    owner = (pair_keep + across(pair_give).astype(F32)).astype(BF)
     owner_all = owner.astype(F32)
     for hop in hops:
         owner_all = owner_all + along(owner, hop).astype(F32)

time: 160 us -> 132 us (0.82)
  starting transfers between devices: 79.7 us -> 59.6 us
  waiting for transfers between devices: 41.1 us -> 24.4 us
  local copies, waits for them, and re-layouts: 5.69 us -> 9.3 us
  Pallas kernels: 20 us -> 23.2 us
  matrix products: 1.23 us -> 3.26 us
    ppermute x18 -> x14, starting transfers between devices: 44.3 us -> 21.6 us  [along(): lax.ppermute(value, 'seq', [(i, (i // CORES + hop) % groups * CORES + i %...]
    ppermute x18 -> x14, waiting for transfers between devices: 41.1 us -> 23.8 us  [along(): lax.ppermute(value, 'seq', [(i, (i // CORES + hop) % groups * CORES + i %...]
    all_to_all x2, starting transfers between devices: 22 us -> 18.2 us  [the longest x1 11.3 us: on_device(): lax.all_to_all(dproj.reshape(plane, 2 * owned, 3 * dim), 'fsdp', 0, 0, ax...]
    ppermute x9, starting transfers between devices: 13.4 us -> 17.1 us  [to_mate(): lax.ppermute(value, 'seq', [(i, i // CORES * CORES + (i + 1) % CORES) for...]
    slice x0 -> x6, local copies, waits for them, and re-layouts: none -> 3.32 us  [the longest x1 0.92 us: on_device(): far_high = along(behind[:, width // 2:], groups - 1)]
    pallas_call x2 -> x3, Pallas kernels: 20 us -> 23.2 us  [the longest x1 10.5 us: on_device(): pl.pallas_call(partial(late_kernel, groups, rows), out_shape=(shape((3, s...]
    ppermute x0 -> x2, starting transfers between devices: none -> 2.69 us  [across(): lax.ppermute(value, 'fsdp', [(i, i + 1 - 2 * (i % 2)) for i in range(devi...]
  transfers between devices with their start and end apart: 29 -> 27, of which waited for: 7 -> 7; matrix products, arithmetic and copies ran while one was open for 9% -> 14% of each run, Pallas kernels for 6% -> 10%
where the time goes in v2:
time: 132 us; the launch traced here: 131 us
  starting transfers between devices  59.6 us (45%)
  waiting for transfers between devices  24.4 us (18%)
  Pallas kernels  23.2 us (18%)
  other arithmetic  10.5 us (8%)
  local copies, waits for them, and re-layouts  9.3 us (7%)
  matrix products  3.26 us (2%)
    ppermute x14, waiting for transfers between devices, along(): lax.ppermute(value, 'seq', [(i, (i // CORES + hop) % groups * CORES + i %...  23.8 us
    ppermute x14, starting transfers between devices, along(): lax.ppermute(value, 'seq', [(i, (i // CORES + hop) % groups * CORES + i %...  21.6 us
    ppermute x9, starting transfers between devices, to_mate(): lax.ppermute(value, 'seq', [(i, i // CORES * CORES + (i + 1) % CORES) for...  17.1 us
    all_to_all x1, starting transfers between devices, on_device(): lax.all_to_all(dproj.reshape(plane, 2 * owned, 3 * dim), 'fsdp', 0, 0, ax...  11.3 us
    pallas_call x1, Pallas kernels, on_device(): pl.pallas_call(partial(late_kernel, groups, rows), out_shape=(shape((3, s...  10.5 us
    pallas_call x1, Pallas kernels, on_device(): pl.pallas_call(partial(update_kernel, groups, rows), out_shape=(shape((3,...  8.37 us
    all_to_all x1, starting transfers between devices, on_device(): lax.all_to_all(jnp.broadcast_to(both, (plane, 2 * owned, 3 * dim)), 'fsdp...  6.89 us
    pallas_call x1, Pallas kernels, on_device(): pl.pallas_call(early_kernel, out_shape=(shape((3, dim, hid), F32), shape(...  4.3 us
  transfers between devices with their start and end apart: 27, of which 7 were waited for; matrix products, arithmetic and copies ran while one was open for 14% of the time, Pallas kernels for 10%

profile of v2, /device:TPU:1, one launch (start us, length us, event | category | flops | bytes accessed | tf_op | source)
XLA Modules:
  0.0 131.3 jit_solution(10773287282339016062)
XLA Ops:
  2.6 3.3 %collective-permute-start.1 = (bf16[272,1024]{1,0:T(8,128)(2,1)S(1)}, bf16[272,1024]{1,0:T(8,128)(2,1)S(1)}, u32[]{:S(2)}, u32[]{:S(2)}) collective-permute-start(bf16[272,1024]{1,0:T(8,128)(2,1)S(1)} %pad_maximum_fusion.1), channel_id=1, source_target_pairs={{0,32},{32,0},{64,96},{96,64},{128,160},{160,128},{192,224},{224,1... | collective-permute-start | bytes 1671176 | tf_op jit(solution)/shard_map/ppermute | solution.py:243
  6.1 5.1 %collective-permute-start.5 = (bf16[144,1024]{1,0:T(8,128)(2,1)S(1)}, bf16[144,1024]{1,0:T(8,128)(2,1)}, u32[]{:S(2)}, u32[]{:S(2)}) collective-permute-start(bf16[144,1024]{1,0:T(8,128)(2,1)S(1)} %pad_maximum_fusion.2.refs_0_.refs_11_), channel_id=1, source_target_pairs={{0,192},{32,224},{64,0},{96,32},{128,64},{160,96},{192,128},{224,1... | collective-permute-start | bytes 884744 | tf_op jit(solution)/shard_map/ppermute | solution.py:248
  12.5 6.9 %all-to-all-start = ((bf16[16,64,768]{2,1,0:T(8,128)(2,1)}), bf16[16,64,768]{2,1,0:T(8,128)(2,1)S(1)}, u32[]{:S(2)}, u32[]{:S(2)}) async-start(bf16[16,64,768]{2,1,0:T(8,128)(2,1)} %broadcast_in_dim.11), calls=%async_computation | async-start | bytes 3145728 | tf_op jit(solution)/shard_map/all_to_all | solution.py:286
  20.4 3.4 %select_bitcast_fusion.refs_11_.state.refs_6_ = f32[3,256,512]{2,1,0:T(8,128)} fusion(f32[1,2,3,256,512]{4,3,2,1,0:T(8,128)} %param.7, pred[]{:T(512)S(6)} %eq.5), kind=kLoop, calls=%fused_computation.3 | loop fusion | flops 393216 | bytes 4718593 | tf_op jit(solution)/shard_map/jit(_where)/select_n | solution.py:275
  26.0 3.9 %collective-permute-start.6 = (bf16[144,512]{1,0:T(8,128)(2,1)S(1)}, bf16[144,512]{1,0:T(8,128)(2,1)S(1)}, u32[]{:S(2)}, u32[]{:S(2)}) collective-permute-start(bf16[144,512]{1,0:T(8,128)(2,1)S(1)} %slice.162), channel_id=1, source_target_pairs={{0,192},{32,224},{64,0},{96,32},{128,64},{160,96},{192,128},{224,1... | collective-permute-start | bytes 442376 | tf_op jit(solution)/shard_map/ppermute | solution.py:248
  32.1 3.6 %collective-permute-done.6.refs_7_ = bf16[144,512]{1,0:T(8,128)(2,1)S(1)} collective-permute-done((bf16[144,512]{1,0:T(8,128)(2,1)S(1)}, bf16[144,512]{1,0:T(8,128)(2,1)S(1)}, u32[]{:S(2)}, u32[]{:S(2)}) %collective-permute-start.6) | collective-permute-done | bytes 147488 | tf_op jit(solution)/shard_map/ppermute | solution.py:248
  36.5 4.5 %collective-permute-done.4.refs_6_ = bf16[144,512]{1,0:T(8,128)(2,1)} collective-permute-done((bf16[144,512]{1,0:T(8,128)(2,1)S(1)}, bf16[144,512]{1,0:T(8,128)(2,1)}, u32[]{:S(2)}, u32[]{:S(2)}) %collective-permute-start.4) | collective-permute-done | bytes 147488 | tf_op jit(solution)/shard_map/ppermute | solution.py:248
  44.0 1.9 %collective-permute-start.7 = (bf16[256,512]{1,0:T(8,128)(2,1)S(1)}, bf16[256,512]{1,0:T(8,128)(2,1)S(1)}, u32[]{:S(2)}, u32[]{:S(2)}) collective-permute-start(bf16[256,512]{1,0:T(8,128)(2,1)S(1)} %maximum_maximum_fusion.refs_0_), channel_id=1, source_target_pairs={{0,64},{32,96},{64,128},{96,160},{128,192},{160,224},{192,0},{224,... | collective-permute-start | bytes 786440 | tf_op jit(solution)/shard_map/ppermute | solution.py:248
  46.6 8.4 %update.1 = (bf16[3,256,512]{2,1,0:T(8,128)(2,1)}, bf16[256,512]{1,0:T(8,128)(2,1)}, f32[1024,128]{1,0:T(8,128)}) custom-call(s32[1]{0:T(128)} %bitcast.1.head_ref, bf16[144,1024]{1,0:T(8,128)(2,1)} %copy-done.7, bf16[144,1024]{1,0:T(8,128)(2,1)} %slice.140.refs_1_.refs_12_, bf16[144,1024]{1,0:T(8,128)(2,1)} %collective-permute-done.3.refs_2_, ...), custom_call_target="tpu_custom_call" | custom-call | flops 8999999488 | bytes 6291456 | tf_op jit(solution)/shard_map/update/pallas_call | solution.py:329
  55.0 1.7 %collective-permute-start.10 = (bf16[256,256]{1,0:T(8,128)(2,1)S(1)}, bf16[256,256]{1,0:T(8,128)(2,1)S(1)}, u32[]{:S(2)}, u32[]{:S(2)}) collective-permute-start(bf16[256,256]{1,0:T(8,128)(2,1)S(1)} %slice.164), channel_id=1, source_target_pairs={{0,192},{32,224},{64,0},{96,32},{128,64},{160,96},{192,128},{224,1... | collective-permute-start | bytes 393224 | tf_op jit(solution)/shard_map/ppermute | solution.py:248
  57.6 4.3 %early.1 = (f32[3,256,512]{2,1,0:T(8,128)}, bf16[256,256]{1,0:T(8,128)(2,1)}) custom-call(bf16[1024,768]{1,0:T(8,128)(2,1)} %bitcast.64, f32[3,256,512]{2,1,0:T(8,128)} %select_bitcast_fusion.refs_11_.state.refs_6_, bf16[128,1024]{1,0:T(8,128)(2,1)} %copy-done.2, bf16[128,1024]{1,0:T(8,128)(2,1)} %get-tuple-element.37.tok_mate, ...), custom_call_target="tpu_custom_call" | custom-call | flops 4000000000 | bytes 6291456 | tf_op jit(solution)/shard_map/early/pallas_call | solution.py:318
  61.9 1.9 %collective-permute-done.9.refs_3_ = bf16[256,256]{1,0:T(8,128)(2,1)S(1)} collective-permute-done((bf16[256,256]{1,0:T(8,128)(2,1)S(1)}, bf16[256,256]{1,0:T(8,128)(2,1)S(1)}, u32[]{:S(2)}, u32[]{:S(2)}) %collective-permute-start.9) | collective-permute-done | bytes 131104 | tf_op jit(solution)/shard_map/ppermute | solution.py:248
  64.5 10.5 %late.1 = (f32[3,64,512]{2,1,0:T(8,128)}, bf16[4,3,64,512]{3,2,1,0:T(8,128)(2,1)}, bf16[1024,768]{1,0:T(8,128)(2,1)}, bf16[256,768]{1,0:T(8,128)(2,1)}, bf16[256,256]{1,0:T(8,128)(2,1)}) custom-call(s32[2]{0:T(128)} %pad_add_fusion.place, bf16[256,512]{1,0:T(8,128)(2,1)} %copy-done.8, bf16[256,512]{1,0:T(8,128)(2,1)} %copy-done.13, ...), custom_call_target="tpu_custom_call" | custom-call | flops 11000000512 | bytes 6291456 | tf_op jit(solution)/shard_map/late/pallas_call | solution.py:349
  75.1 11.3 %all-to-all-start.1 = ((bf16[16,64,768]{2,1,0:T(8,128)(2,1)}), bf16[16,64,768]{2,1,0:T(8,128)(2,1)}, u32[]{:S(2)}, u32[]{:S(2)}) async-start(bf16[16,64,768]{2,1,0:T(8,128)(2,1)} %bitcast.67), calls=%async_computation.1 | async-start | bytes 3145728 | tf_op jit(solution)/shard_map/all_to_all | solution.py:383
  86.5 3.6 %collective-permute-start.18 = (bf16[3,64,512]{2,1,0:T(8,128)(2,1)S(1)}, bf16[3,64,512]{2,1,0:T(8,128)(2,1)S(1)}, u32[]{:S(2)}, u32[]{:S(2)}) collective-permute-start(bf16[3,64,512]{2,1,0:T(8,128)(2,1)S(1)} %get-tuple-element.35), channel_id=1, source_target_pairs={{0,192},{32,224},{64,0},{96,32},{128,64},{160,96},{192,128},{224,1... | collective-permute-start | bytes 589832 | tf_op jit(solution)/shard_map/ppermute | solution.py:248
  94.0 2.5 %collective-permute-start.15 = (bf16[2,128,1024]{2,1,0:T(8,128)(2,1)}, bf16[2,128,1024]{2,1,0:T(8,128)(2,1)}, u32[]{:S(2)}, u32[]{:S(2)}) collective-permute-start(bf16[2,128,1024]{2,1,0:T(8,128)(2,1)} %fusion.3), channel_id=1, source_target_pairs={{0,32},{32,0},{64,96},{96,64},{128,160},{160,128},{192,224},{224,1... | collective-permute-start | bytes 1572872 | tf_op jit(solution)/shard_map/ppermute | solution.py:243
  96.5 9.5 %collective-permute-done.17 = bf16[3,64,512]{2,1,0:T(8,128)(2,1)S(1)} collective-permute-done((bf16[3,64,512]{2,1,0:T(8,128)(2,1)S(1)}, bf16[3,64,512]{2,1,0:T(8,128)(2,1)S(1)}, u32[]{:S(2)}, u32[]{:S(2)}) %collective-permute-start.17) | collective-permute-done | bytes 196640 | tf_op jit(solution)/shard_map/ppermute | solution.py:248
  108.4 2.6 %collective-permute-start.20 = (bf16[32,768]{1,0:T(8,128)(2,1)S(1)}, bf16[32,768]{1,0:T(8,128)(2,1)S(1)}, u32[]{:S(2)}, u32[]{:S(2)}) collective-permute-start(bf16[32,768]{1,0:T(8,128)(2,1)S(1)} %select_convert_fusion), channel_id=1, source_target_pairs={{0,1},{1,0},{2,3},{3,2},{4,5},{5,4},{6,7},{7,6},{8,9},{9,8},{10,11... | collective-permute-start | bytes 147464 | tf_op jit(solution)/shard_map/ppermute | solution.py:262
  111.1 4.6 %collective-permute-start.19 = (f32[3,32,512]{2,1,0:T(8,128)S(1)}, f32[3,32,512]{2,1,0:T(8,128)S(1)}, u32[]{:S(2)}, u32[]{:S(2)}) collective-permute-start(f32[3,32,512]{2,1,0:T(8,128)S(1)} %get-tuple-element.42), channel_id=1, source_target_pairs={{0,32},{32,0},{64,96},{96,64},{128,160},{160,128},{192,224},{224,1... | collective-permute-start | bytes 589832 | tf_op jit(solution)/shard_map/ppermute | solution.py:243
  115.8 3.8 %collective-permute-start.22 = (bf16[32,768]{1,0:T(8,128)(2,1)S(1)}, bf16[32,768]{1,0:T(8,128)(2,1)S(1)}, u32[]{:S(2)}, u32[]{:S(2)}) collective-permute-start(bf16[32,768]{1,0:T(8,128)(2,1)S(1)} %add_convert_fusion), channel_id=1, source_target_pairs={{0,128},{32,160},{64,192},{96,224},{128,0},{160,32},{192,64},{224,... | collective-permute-start | bytes 147464 | tf_op jit(solution)/shard_map/ppermute | solution.py:248
  120.3 2.4 %collective-permute-done.22 = bf16[32,768]{1,0:T(8,128)(2,1)S(1)} collective-permute-done((bf16[32,768]{1,0:T(8,128)(2,1)S(1)}, bf16[32,768]{1,0:T(8,128)(2,1)S(1)}, u32[]{:S(2)}, u32[]{:S(2)}) %collective-permute-start.22) | collective-permute-done | bytes 49184 | tf_op jit(solution)/shard_map/ppermute | solution.py:248
  122.7 1.8 %collective-permute-done.21 = bf16[32,768]{1,0:T(8,128)(2,1)S(1)} collective-permute-done((bf16[32,768]{1,0:T(8,128)(2,1)S(1)}, bf16[32,768]{1,0:T(8,128)(2,1)S(1)}, u32[]{:S(2)}, u32[]{:S(2)}) %collective-permute-start.21) | collective-permute-done | bytes 49184 | tf_op jit(solution)/shard_map/ppermute | solution.py:248
  124.6 3.7 %collective-permute-start.24 = (f32[32,768]{1,0:T(8,128)S(1)}, f32[32,768]{1,0:T(8,128)S(1)}, u32[]{:S(2)}, u32[]{:S(2)}) collective-permute-start(f32[32,768]{1,0:T(8,128)S(1)} %convert_add_fusion.1), channel_id=1, source_target_pairs={{0,32},{32,0},{64,96},{96,64},{128,160},{160,128},{192,224},{224,1... | collective-permute-start | bytes 294920 | tf_op jit(solution)/shard_map/ppermute | solution.py:243
  128.4 2.0 %fusion.4 = bf16[1,2,128,1024]{3,2,1,0:T(8,128)(2,1)} fusion(bf16[2,128,1024]{2,1,0:T(8,128)(2,1)} %collective-permute-done.15, f32[1,256,1024]{2,1,0:T(8,128)S(1)} %convolution_bitcast_fusion, f32[1,256,1024]{2,1,0:T(8,128)S(1)} %convolution_bitcast_fusion.1), kind=kLoop, calls=%fused_computation.13 | loop fusion | flops 1048576 | bytes 3145728 | tf_op jit(solution)/shard_map/broadcast_in_dim | solution.py:424
  (112 shorter events, 22.9 us)
Async XLA Ops:
  2.6 8.6 %collective-permute-start.1 = (bf16[272,1024]{1,0:T(8,128)(2,1)S(1)}, bf16[272,1024]{1,0:T(8,128)(2,1)S(1)}, u32[]{:S(2)}, u32[]{:S(2)}) collective-permute-start(bf16[272,1024]{1,0:T(8,128)(2,1)S(1)} %pad_maximum_fusion.1), channel_id=1, source_target_pairs={{0,32},{32,0},{64,96},{96,64},{128,160},{160,128},{192,224},{224,1... | collective-permute-start | bytes 1671176 | tf_op jit(solution)/shard_map/ppermute | solution.py:243
  5.9 5.2 %collective-permute-start = (bf16[32,768]{1,0:T(8,128)(2,1)S(1)}, bf16[32,768]{1,0:T(8,128)(2,1)S(1)}, u32[]{:S(2)}, u32[]{:S(2)}) collective-permute-start(bf16[32,768]{1,0:T(8,128)(2,1)S(1)} %bitcast.69), channel_id=1, source_target_pairs={{0,1},{1,0},{2,3},{3,2},{4,5},{5,4},{6,7},{7,6},{8,9},{9,8},{10,11... | collective-permute-start | bytes 147464 | tf_op jit(solution)/shard_map/ppermute | solution.py:262
  6.1 19.0 %collective-permute-start.5 = (bf16[144,1024]{1,0:T(8,128)(2,1)S(1)}, bf16[144,1024]{1,0:T(8,128)(2,1)}, u32[]{:S(2)}, u32[]{:S(2)}) collective-permute-start(bf16[144,1024]{1,0:T(8,128)(2,1)S(1)} %pad_maximum_fusion.2.refs_0_.refs_11_), channel_id=1, source_target_pairs={{0,192},{32,224},{64,0},{96,32},{128,64},{160,96},{192,128},{224,1... | collective-permute-start | bytes 884744 | tf_op jit(solution)/shard_map/ppermute | solution.py:248
  11.1 18.8 %collective-permute-start.3 = (bf16[144,1024]{1,0:T(8,128)(2,1)S(1)}, bf16[144,1024]{1,0:T(8,128)(2,1)}, u32[]{:S(2)}, u32[]{:S(2)}) collective-permute-start(bf16[144,1024]{1,0:T(8,128)(2,1)S(1)} %pad_maximum_fusion.2.refs_0_.refs_11_), channel_id=1, source_target_pairs={{0,64},{32,96},{64,128},{96,160},{128,192},{160,224},{192,0},{224,... | collective-permute-start | bytes 884744 | tf_op jit(solution)/shard_map/ppermute | solution.py:248
  12.5 30.6 %all-to-all-start = ((bf16[16,64,768]{2,1,0:T(8,128)(2,1)}), bf16[16,64,768]{2,1,0:T(8,128)(2,1)S(1)}, u32[]{:S(2)}, u32[]{:S(2)}) async-start(bf16[16,64,768]{2,1,0:T(8,128)(2,1)} %broadcast_in_dim.11), calls=%async_computation | async-start | bytes 3145728 | tf_op jit(solution)/shard_map/all_to_all | solution.py:286
  19.4 11.5 %collective-permute-start.2 = (bf16[2,128,256]{2,1,0:T(8,128)(2,1)S(1)}, bf16[2,128,256]{2,1,0:T(8,128)(2,1)S(1)}, u32[]{:S(2)}, u32[]{:S(2)}) collective-permute-start(bf16[2,128,256]{2,1,0:T(8,128)(2,1)S(1)} %select_bitcast_fusion.2), channel_id=1, source_target_pairs={{0,32},{32,0},{64,96},{96,64},{128,160},{160,128},{192,224},{224,1... | collective-permute-start | bytes 393224 | tf_op jit(solution)/shard_map/ppermute | solution.py:243
  26.0 9.7 %collective-permute-start.6 = (bf16[144,512]{1,0:T(8,128)(2,1)S(1)}, bf16[144,512]{1,0:T(8,128)(2,1)S(1)}, u32[]{:S(2)}, u32[]{:S(2)}) collective-permute-start(bf16[144,512]{1,0:T(8,128)(2,1)S(1)} %slice.162), channel_id=1, source_target_pairs={{0,192},{32,224},{64,0},{96,32},{128,64},{160,96},{192,128},{224,1... | collective-permute-start | bytes 442376 | tf_op jit(solution)/shard_map/ppermute | solution.py:248
  30.9 10.1 %collective-permute-start.4 = (bf16[144,512]{1,0:T(8,128)(2,1)S(1)}, bf16[144,512]{1,0:T(8,128)(2,1)}, u32[]{:S(2)}, u32[]{:S(2)}) collective-permute-start(bf16[144,512]{1,0:T(8,128)(2,1)S(1)} %slice.161), channel_id=1, source_target_pairs={{0,64},{32,96},{64,128},{96,160},{128,192},{160,224},{192,0},{224,... | collective-permute-start | bytes 442376 | tf_op jit(solution)/shard_map/ppermute | solution.py:248
  31.6 14.3 %collective-permute-start.12 = (bf16[144,1024]{1,0:T(8,128)(2,1)}, bf16[144,1024]{1,0:T(8,128)(2,1)S(1)}, u32[]{:S(2)}, u32[]{:S(2)}) collective-permute-start(bf16[144,1024]{1,0:T(8,128)(2,1)} %collective-permute-done.5.refs_4_), channel_id=1, source_target_pairs={{0,32},{32,0},{64,96},{96,64},{128,160},{160,128},{192,224},{224,1... | collective-permute-start | bytes 884744 | tf_op jit(solution)/shard_map/ppermute | solution.py:243
  32.0 13.9 %collective-permute-start.11 = (bf16[144,1024]{1,0:T(8,128)(2,1)}, bf16[144,1024]{1,0:T(8,128)(2,1)}, u32[]{:S(2)}, u32[]{:S(2)}) collective-permute-start(bf16[144,1024]{1,0:T(8,128)(2,1)} %collective-permute-done.3.refs_2_), channel_id=1, source_target_pairs={{0,32},{32,0},{64,96},{96,64},{128,160},{160,128},{192,224},{224,1... | collective-permute-start | bytes 884744 | tf_op jit(solution)/shard_map/ppermute | solution.py:243
  35.7 8.3 %collective-permute-start.14 = (bf16[144,512]{1,0:T(8,128)(2,1)S(1)}, bf16[144,512]{1,0:T(8,128)(2,1)}, u32[]{:S(2)}, u32[]{:S(2)}) collective-permute-start(bf16[144,512]{1,0:T(8,128)(2,1)S(1)} %collective-permute-done.6.refs_7_), channel_id=1, source_target_pairs={{0,32},{32,0},{64,96},{96,64},{128,160},{160,128},{192,224},{224,1... | collective-permute-start | bytes 442376 | tf_op jit(solution)/shard_map/ppermute | solution.py:243
  43.4 11.6 %collective-permute-start.8 = (bf16[256,512]{1,0:T(8,128)(2,1)S(1)}, bf16[256,512]{1,0:T(8,128)(2,1)S(1)}, u32[]{:S(2)}, u32[]{:S(2)}) collective-permute-start(bf16[256,512]{1,0:T(8,128)(2,1)S(1)} %maximum_maximum_fusion.refs_0_), channel_id=1, source_target_pairs={{0,192},{32,224},{64,0},{96,32},{128,64},{160,96},{192,128},{224,1... | collective-permute-start | bytes 786440 | tf_op jit(solution)/shard_map/ppermute | solution.py:248
  44.0 12.8 %collective-permute-start.7 = (bf16[256,512]{1,0:T(8,128)(2,1)S(1)}, bf16[256,512]{1,0:T(8,128)(2,1)S(1)}, u32[]{:S(2)}, u32[]{:S(2)}) collective-permute-start(bf16[256,512]{1,0:T(8,128)(2,1)S(1)} %maximum_maximum_fusion.refs_0_), channel_id=1, source_target_pairs={{0,64},{32,96},{64,128},{96,160},{128,192},{160,224},{192,0},{224,... | collective-permute-start | bytes 786440 | tf_op jit(solution)/shard_map/ppermute | solution.py:248
  55.0 6.8 %collective-permute-start.10 = (bf16[256,256]{1,0:T(8,128)(2,1)S(1)}, bf16[256,256]{1,0:T(8,128)(2,1)S(1)}, u32[]{:S(2)}, u32[]{:S(2)}) collective-permute-start(bf16[256,256]{1,0:T(8,128)(2,1)S(1)} %slice.164), channel_id=1, source_target_pairs={{0,192},{32,224},{64,0},{96,32},{128,64},{160,96},{192,128},{224,1... | collective-permute-start | bytes 393224 | tf_op jit(solution)/shard_map/ppermute | solution.py:248
  56.8 7.1 %collective-permute-start.9 = (bf16[256,256]{1,0:T(8,128)(2,1)S(1)}, bf16[256,256]{1,0:T(8,128)(2,1)S(1)}, u32[]{:S(2)}, u32[]{:S(2)}) collective-permute-start(bf16[256,256]{1,0:T(8,128)(2,1)S(1)} %slice.163), channel_id=1, source_target_pairs={{0,64},{32,96},{64,128},{96,160},{128,192},{160,224},{192,0},{224,... | collective-permute-start | bytes 393224 | tf_op jit(solution)/shard_map/ppermute | solution.py:248
  75.1 31.7 %all-to-all-start.1 = ((bf16[16,64,768]{2,1,0:T(8,128)(2,1)}), bf16[16,64,768]{2,1,0:T(8,128)(2,1)}, u32[]{:S(2)}, u32[]{:S(2)}) async-start(bf16[16,64,768]{2,1,0:T(8,128)(2,1)} %bitcast.67), calls=%async_computation.1 | async-start | bytes 3145728 | tf_op jit(solution)/shard_map/all_to_all | solution.py:383
  86.4 10.1 %collective-permute-start.16 = (bf16[3,64,512]{2,1,0:T(8,128)(2,1)S(1)}, bf16[3,64,512]{2,1,0:T(8,128)(2,1)S(1)}, u32[]{:S(2)}, u32[]{:S(2)}) collective-permute-start(bf16[3,64,512]{2,1,0:T(8,128)(2,1)S(1)} %get-tuple-element.34), channel_id=1, source_target_pairs={{0,64},{32,96},{64,128},{96,160},{128,192},{160,224},{192,0},{224,... | collective-permute-start | bytes 589832 | tf_op jit(solution)/shard_map/ppermute | solution.py:248
  86.5 10.0 %collective-permute-start.18 = (bf16[3,64,512]{2,1,0:T(8,128)(2,1)S(1)}, bf16[3,64,512]{2,1,0:T(8,128)(2,1)S(1)}, u32[]{:S(2)}, u32[]{:S(2)}) collective-permute-start(bf16[3,64,512]{2,1,0:T(8,128)(2,1)S(1)} %get-tuple-element.35), channel_id=1, source_target_pairs={{0,192},{32,224},{64,0},{96,32},{128,64},{160,96},{192,128},{224,1... | collective-permute-start | bytes 589832 | tf_op jit(solution)/shard_map/ppermute | solution.py:248
  90.1 16.0 %collective-permute-start.17 = (bf16[3,64,512]{2,1,0:T(8,128)(2,1)S(1)}, bf16[3,64,512]{2,1,0:T(8,128)(2,1)S(1)}, u32[]{:S(2)}, u32[]{:S(2)}) collective-permute-start(bf16[3,64,512]{2,1,0:T(8,128)(2,1)S(1)} %get-tuple-element.36), channel_id=1, source_target_pairs={{0,128},{32,160},{64,192},{96,224},{128,0},{160,32},{192,64},{224,... | collective-permute-start | bytes 589832 | tf_op jit(solution)/shard_map/ppermute | solution.py:248
  94.0 34.4 %collective-permute-start.15 = (bf16[2,128,1024]{2,1,0:T(8,128)(2,1)}, bf16[2,128,1024]{2,1,0:T(8,128)(2,1)}, u32[]{:S(2)}, u32[]{:S(2)}) collective-permute-start(bf16[2,128,1024]{2,1,0:T(8,128)(2,1)} %fusion.3), channel_id=1, source_target_pairs={{0,32},{32,0},{64,96},{96,64},{128,160},{160,128},{192,224},{224,1... | collective-permute-start | bytes 1572872 | tf_op jit(solution)/shard_map/ppermute | solution.py:243
  108.4 7.2 %collective-permute-start.20 = (bf16[32,768]{1,0:T(8,128)(2,1)S(1)}, bf16[32,768]{1,0:T(8,128)(2,1)S(1)}, u32[]{:S(2)}, u32[]{:S(2)}) collective-permute-start(bf16[32,768]{1,0:T(8,128)(2,1)S(1)} %select_convert_fusion), channel_id=1, source_target_pairs={{0,1},{1,0},{2,3},{3,2},{4,5},{5,4},{6,7},{7,6},{8,9},{9,8},{10,11... | collective-permute-start | bytes 147464 | tf_op jit(solution)/shard_map/ppermute | solution.py:262
  111.1 8.5 %collective-permute-start.19 = (f32[3,32,512]{2,1,0:T(8,128)S(1)}, f32[3,32,512]{2,1,0:T(8,128)S(1)}, u32[]{:S(2)}, u32[]{:S(2)}) collective-permute-start(f32[3,32,512]{2,1,0:T(8,128)S(1)} %get-tuple-element.42), channel_id=1, source_target_pairs={{0,32},{32,0},{64,96},{96,64},{128,160},{160,128},{192,224},{224,1... | collective-permute-start | bytes 589832 | tf_op jit(solution)/shard_map/ppermute | solution.py:243
  115.8 7.0 %collective-permute-start.22 = (bf16[32,768]{1,0:T(8,128)(2,1)S(1)}, bf16[32,768]{1,0:T(8,128)(2,1)S(1)}, u32[]{:S(2)}, u32[]{:S(2)}) collective-permute-start(bf16[32,768]{1,0:T(8,128)(2,1)S(1)} %add_convert_fusion), channel_id=1, source_target_pairs={{0,128},{32,160},{64,192},{96,224},{128,0},{160,32},{192,64},{224,... | collective-permute-start | bytes 147464 | tf_op jit(solution)/shard_map/ppermute | solution.py:248
  124.6 5.8 %collective-permute-start.24 = (f32[32,768]{1,0:T(8,128)S(1)}, f32[32,768]{1,0:T(8,128)S(1)}, u32[]{:S(2)}, u32[]{:S(2)}) collective-permute-start(f32[32,768]{1,0:T(8,128)S(1)} %convert_add_fusion.1), channel_id=1, source_target_pairs={{0,32},{32,0},{64,96},{96,64},{128,160},{160,128},{192,224},{224,1... | collective-permute-start | bytes 294920 | tf_op jit(solution)/shard_map/ppermute | solution.py:243
  (21 other events, 177.9 us)

commit v3 on v2

--- a/solution.py
+++ b/solution.py
@@ -101,27 +101,33 @@
 def update_kernel(count, rows, head_ref, *refs):
     refs = list(refs)
     pieces = piece_refs(refs[: 2 * count + 2], count)
-    whole, state, next_ref, kv_ref, rate_ref, keys, w16, total = refs[2 * count + 2 :]
+    whole, state, next_ref, kv_ref, rate_ref, keys, rate_all, w16, total = refs[2 * count + 2 :]
     dim = state.shape[1]
     half = whole.shape[0] // 2
     head = head_ref[0]
     for part in range(3):
         w16[part] = state[part].astype(BF)
         total[part] = state[part]
+    group = len(pieces) // 2
+    for first in range(0, len(pieces), group):
+        some = pieces[first : first + group]
+        low = jnp.concatenate([piece[0][:rows, :] for piece in some], axis=0)
+        high = jnp.concatenate([piece[1][:rows, :] for piece in some], axis=0)
+        out = dot_nn(low, whole[:half, dim:]) + dot_nn(high, whole[half:, dim:])
+        keys[first * rows : (first + group) * rows, :] = out.astype(BF)
     for index, piece in enumerate(pieces):
-        out = dot_nn(piece[0][:rows, :], whole[:half, dim:])
-        out = out + dot_nn(piece[1][:rows, :], whole[half:, dim:])
-        keys[index * rows : (index + 1) * rows, :] = out.astype(BF)
-        rate_ref[index * rows : (index + 1) * rows, :] = jnp.broadcast_to(
-            piece_rate(piece, rows, head), (rows, rate_ref.shape[1])
+        rate_all[index * rows : (index + 1) * rows, :] = jnp.broadcast_to(
+            piece_rate(piece, rows, head), (rows, rate_all.shape[1])
         )
     span = CORES * rows
     kv_ref[...] = keys[:span, :]
+    rate_ref[...] = rate_all[:span, :]
+    block_rows = group * rows
 
     def step(block, carry):
-        at = pl.ds(pl.multiple_of(block * span, span), span)
+        at = pl.ds(pl.multiple_of(block * block_rows, block_rows), block_rows)
         pair = keys[at, :].astype(F32)
-        rate = rate_ref[at, :1]
+        rate = rate_all[at, :1]
         key = pair[:, :dim]
         unit16 = (key * inverse_rms(key)).astype(BF)
         cot = (pair[:, dim:] * rate).astype(BF)
@@ -131,7 +137,7 @@
         total[2] += dot_tn(cot, hidden)
         return carry
 
-    lax.fori_loop(0, count, step, 0)
+    lax.fori_loop(0, 2, step, 0)
     for part in range(3):
         next_ref[part] = total[part].astype(BF)
 
@@ -150,21 +156,22 @@
     share = dim // count
     for part in range(3):
         w16[part] = state[part].astype(BF)
-        total[part] = jnp.zeros_like(total[part])
     late = (next_w[0], next_w[1], next_w[2])
-    for block in range(count):
-        query = queries[block][...].astype(F32)
+    for block in range(2):
+        size = count // 2
+        picks = range(block * size, (block + 1) * size)
+        query = jnp.concatenate([queries[i][...] for i in picks], axis=0).astype(F32)
         scale = inverse_rms(query)
         unit = query * scale
         unit16 = unit.astype(BF)
-        cot = cots[block][...]
+        cot = jnp.concatenate([cots[i][...] for i in picks], axis=0)
         d_gate, d_up, hidden = weight_terms(unit16, cot, late)
-        total[0] += dot_tn(unit16, d_gate)
-        total[1] += dot_tn(unit16, d_up)
-        total[2] += dot_tn(cot, hidden)
+        terms = (dot_tn(unit16, d_gate), dot_tn(unit16, d_up), dot_tn(cot, hidden))
+        for part in range(3):
+            total[part] = terms[part] if block == 0 else total[part] + terms[part]
         if block == 0:
-            pulled = dot_nt(d_gate, late[0]) + dot_nt(d_up, late[1])
-            g1_ref[...] = unit_pull(pulled, unit, scale).astype(BF)
+            pulled = dot_nt(d_gate[:span], late[0]) + dot_nt(d_up[:span], late[1])
+            g1_ref[...] = unit_pull(pulled, unit[:span], scale[:span]).astype(BF)
     for part in range(3):
         c16[part] = total[part].astype(BF)
     start = pl.multiple_of(place[0] * share, share)
@@ -331,12 +338,13 @@
         out_shape=(
             shape((3, dim, hid), BF),
             shape((span, 2 * dim), BF),
-            shape((groups * span, 128), F32),
+            shape((span, 128), F32),
         ),
         in_specs=[SMEM] + [VMEM] * (2 * groups + 4),
         out_specs=(VMEM,) * 3,
         scratch_shapes=[
             pltpu.VMEM((groups * span, 2 * dim), BF),
+            pltpu.VMEM((groups * span, 128), F32),
             pltpu.VMEM((3, dim, hid), BF),
             pltpu.VMEM((3, dim, hid), F32),
         ],
@@ -395,15 +403,6 @@
     owner_all = owner.astype(F32)
     for hop in hops:
         owner_all = owner_all + along(owner, hop).astype(F32)
-    owner_mate = to_mate(owner_all)
-    owner_all = owner_all.reshape(owned, 3, dim)
-    owner_mate = owner_mate.reshape(owned, 3, dim)
-    d_proj = jnp.where(
-        core == 0,
-        jnp.concatenate([owner_all, owner_mate], axis=-1),
-        jnp.concatenate([owner_mate, owner_all], axis=-1),
-    )
-
     summed = carried + shares[0].astype(F32)
     for hop in hops:
         summed = summed + along(shares[hop], hop).astype(F32)
@@ -422,6 +421,16 @@
     part = jnp.stack([part0, part1])
     from_mate = to_mate(part[:, rows:].astype(BF))
     d_tokens = (part[:, :rows] + from_mate.astype(F32)).astype(BF)[None]
+    owner_all, d_state, d_tokens = lax.optimization_barrier((owner_all, d_state, d_tokens))
+    owner_mate = to_mate(owner_all)
+    owner_all = owner_all.reshape(owned, 3, dim)
+    owner_mate = owner_mate.reshape(owned, 3, dim)
+    d_proj = jnp.where(
+        core == 0,
+        jnp.concatenate([owner_all, owner_mate], axis=-1),
+        jnp.concatenate([owner_mate, owner_all], axis=-1),
+    )
+
     return (d_tokens, d_state, d_proj)
 
 

time: 132 us -> 131 us (level)
  waiting for transfers between devices: 24.4 us -> 21.7 us
  starting transfers between devices: 59.6 us -> 62.1 us
    ppermute x14, waiting for transfers between devices: 23.8 us -> 19.8 us  [along(): lax.ppermute(value, 'seq', [(i, (i // CORES + hop) % groups * CORES + i %...]
    ppermute x14, starting transfers between devices: 21.6 us -> 24.2 us  [along(): lax.ppermute(value, 'seq', [(i, (i // CORES + hop) % groups * CORES + i %...]
    ppermute x9, starting transfers between devices: 17.1 us -> 14.5 us  [to_mate(): lax.ppermute(value, 'seq', [(i, i // CORES * CORES + (i + 1) % CORES) for...]
    ppermute x2, starting transfers between devices: 2.69 us -> 4.28 us  [across(): lax.ppermute(value, 'fsdp', [(i, i + 1 - 2 * (i % 2)) for i in range(devi...]
  transfers between devices with their start and end apart: 27 -> 27, of which waited for: 7 -> 9; matrix products, arithmetic and copies ran while one was open for 14% -> 15% of each run, Pallas kernels for 10% -> 9%
where the time goes in v3:
time: 131 us; the launch traced here: 130 us
  starting transfers between devices  62.1 us (47%)
  Pallas kernels  22.2 us (17%)
  waiting for transfers between devices  21.7 us (17%)
  other arithmetic  10.4 us (8%)
  local copies, waits for them, and re-layouts  9.32 us (7%)
  matrix products  3.27 us (2%)
    ppermute x14, starting transfers between devices, along(): lax.ppermute(value, 'seq', [(i, (i // CORES + hop) % groups * CORES + i %...  24.2 us
    ppermute x14, waiting for transfers between devices, along(): lax.ppermute(value, 'seq', [(i, (i // CORES + hop) % groups * CORES + i %...  19.8 us
    ppermute x9, starting transfers between devices, to_mate(): lax.ppermute(value, 'seq', [(i, i // CORES * CORES + (i + 1) % CORES) for...  14.5 us
    all_to_all x1, starting transfers between devices, on_device(): lax.all_to_all(dproj.reshape(plane, 2 * owned, 3 * dim), 'fsdp', 0, 0, ax...  12.1 us
    pallas_call x1, Pallas kernels, on_device(): pl.pallas_call(partial(late_kernel, groups, rows), out_shape=(shape((3, s...  10.1 us
    pallas_call x1, Pallas kernels, on_device(): pl.pallas_call(partial(update_kernel, groups, rows), out_shape=(shape((3,...  7.75 us
    all_to_all x1, starting transfers between devices, on_device(): lax.all_to_all(jnp.broadcast_to(both, (plane, 2 * owned, 3 * dim)), 'fsdp...  6.89 us
    pallas_call x1, Pallas kernels, on_device(): pl.pallas_call(early_kernel, out_shape=(shape((3, dim, hid), F32), shape(...  4.35 us
  transfers between devices with their start and end apart: 27, of which 9 were waited for; matrix products, arithmetic and copies ran while one was open for 15% of the time, Pallas kernels for 9%

profile of v3, /device:TPU:1, one launch (start us, length us, event | category | flops | bytes accessed | tf_op | source)
XLA Modules:
  0.0 130.0 jit_solution(4835494070068417951)
XLA Ops:
  2.6 3.3 %collective-permute-start.1 = (bf16[272,1024]{1,0:T(8,128)(2,1)S(1)}, bf16[272,1024]{1,0:T(8,128)(2,1)S(1)}, u32[]{:S(2)}, u32[]{:S(2)}) collective-permute-start(bf16[272,1024]{1,0:T(8,128)(2,1)S(1)} %pad_maximum_fusion.1), channel_id=1, source_target_pairs={{0,32},{32,0},{64,96},{96,64},{128,160},{160,128},{192,224},{224,1... | collective-permute-start | bytes 1671176 | tf_op jit(solution)/shard_map/ppermute | solution.py:250
  6.1 5.1 %collective-permute-start.5 = (bf16[144,1024]{1,0:T(8,128)(2,1)S(1)}, bf16[144,1024]{1,0:T(8,128)(2,1)}, u32[]{:S(2)}, u32[]{:S(2)}) collective-permute-start(bf16[144,1024]{1,0:T(8,128)(2,1)S(1)} %pad_maximum_fusion.2.refs_0_.refs_11_), channel_id=1, source_target_pairs={{0,192},{32,224},{64,0},{96,32},{128,64},{160,96},{192,128},{224,1... | collective-permute-start | bytes 884744 | tf_op jit(solution)/shard_map/ppermute | solution.py:255
  12.5 6.9 %all-to-all-start = ((bf16[16,64,768]{2,1,0:T(8,128)(2,1)}), bf16[16,64,768]{2,1,0:T(8,128)(2,1)S(1)}, u32[]{:S(2)}, u32[]{:S(2)}) async-start(bf16[16,64,768]{2,1,0:T(8,128)(2,1)} %broadcast_in_dim.11), calls=%async_computation | async-start | bytes 3145728 | tf_op jit(solution)/shard_map/all_to_all | solution.py:293
  20.4 3.4 %select_bitcast_fusion.refs_11_.state.refs_6_ = f32[3,256,512]{2,1,0:T(8,128)} fusion(f32[1,2,3,256,512]{4,3,2,1,0:T(8,128)} %param.7, pred[]{:T(512)S(6)} %eq.5), kind=kLoop, calls=%fused_computation.3 | loop fusion | flops 393216 | bytes 4718593 | tf_op jit(solution)/shard_map/jit(_where)/select_n | solution.py:282
  26.0 3.9 %collective-permute-start.6 = (bf16[144,512]{1,0:T(8,128)(2,1)S(1)}, bf16[144,512]{1,0:T(8,128)(2,1)S(1)}, u32[]{:S(2)}, u32[]{:S(2)}) collective-permute-start(bf16[144,512]{1,0:T(8,128)(2,1)S(1)} %slice.162), channel_id=1, source_target_pairs={{0,192},{32,224},{64,0},{96,32},{128,64},{160,96},{192,128},{224,1... | collective-permute-start | bytes 442376 | tf_op jit(solution)/shard_map/ppermute | solution.py:255
  32.1 3.6 %collective-permute-done.6.refs_7_ = bf16[144,512]{1,0:T(8,128)(2,1)S(1)} collective-permute-done((bf16[144,512]{1,0:T(8,128)(2,1)S(1)}, bf16[144,512]{1,0:T(8,128)(2,1)S(1)}, u32[]{:S(2)}, u32[]{:S(2)}) %collective-permute-start.6) | collective-permute-done | bytes 147488 | tf_op jit(solution)/shard_map/ppermute | solution.py:255
  36.5 4.5 %collective-permute-done.4.refs_6_ = bf16[144,512]{1,0:T(8,128)(2,1)} collective-permute-done((bf16[144,512]{1,0:T(8,128)(2,1)S(1)}, bf16[144,512]{1,0:T(8,128)(2,1)}, u32[]{:S(2)}, u32[]{:S(2)}) %collective-permute-start.4) | collective-permute-done | bytes 147488 | tf_op jit(solution)/shard_map/ppermute | solution.py:255
  44.0 2.0 %collective-permute-start.7 = (bf16[256,512]{1,0:T(8,128)(2,1)S(1)}, bf16[256,512]{1,0:T(8,128)(2,1)S(1)}, u32[]{:S(2)}, u32[]{:S(2)}) collective-permute-start(bf16[256,512]{1,0:T(8,128)(2,1)S(1)} %maximum_maximum_fusion.refs_0_), channel_id=1, source_target_pairs={{0,64},{32,96},{64,128},{96,160},{128,192},{160,224},{192,0},{224,... | collective-permute-start | bytes 786440 | tf_op jit(solution)/shard_map/ppermute | solution.py:255
  46.6 7.7 %update.1 = (bf16[3,256,512]{2,1,0:T(8,128)(2,1)}, bf16[256,512]{1,0:T(8,128)(2,1)}, f32[256,128]{1,0:T(8,128)}) custom-call(s32[1]{0:T(128)} %bitcast.1.head_ref, bf16[144,1024]{1,0:T(8,128)(2,1)} %copy-done.7, bf16[144,1024]{1,0:T(8,128)(2,1)} %slice.140.refs_1_.refs_12_, bf16[144,1024]{1,0:T(8,128)(2,1)} %collective-permute-done.3.refs_2_, ...), custom_call_target="tpu_custom_call" | custom-call | flops 8999999488 | bytes 6291456 | tf_op jit(solution)/shard_map/update/pallas_call | solution.py:336
  54.4 1.7 %collective-permute-start.10 = (bf16[256,256]{1,0:T(8,128)(2,1)S(1)}, bf16[256,256]{1,0:T(8,128)(2,1)S(1)}, u32[]{:S(2)}, u32[]{:S(2)}) collective-permute-start(bf16[256,256]{1,0:T(8,128)(2,1)S(1)} %slice.164), channel_id=1, source_target_pairs={{0,192},{32,224},{64,0},{96,32},{128,64},{160,96},{192,128},{224,1... | collective-permute-start | bytes 393224 | tf_op jit(solution)/shard_map/ppermute | solution.py:255
  57.0 4.4 %early.1 = (f32[3,256,512]{2,1,0:T(8,128)}, bf16[256,256]{1,0:T(8,128)(2,1)}) custom-call(bf16[1024,768]{1,0:T(8,128)(2,1)} %bitcast.64, f32[3,256,512]{2,1,0:T(8,128)} %select_bitcast_fusion.refs_11_.state.refs_6_, bf16[128,1024]{1,0:T(8,128)(2,1)} %copy-done.2, bf16[128,1024]{1,0:T(8,128)(2,1)} %get-tuple-element.43.tok_mate, ...), custom_call_target="tpu_custom_call" | custom-call | flops 4000000000 | bytes 6291456 | tf_op jit(solution)/shard_map/early/pallas_call | solution.py:325
  61.3 2.2 %collective-permute-done.9.refs_3_ = bf16[256,256]{1,0:T(8,128)(2,1)S(1)} collective-permute-done((bf16[256,256]{1,0:T(8,128)(2,1)S(1)}, bf16[256,256]{1,0:T(8,128)(2,1)S(1)}, u32[]{:S(2)}, u32[]{:S(2)}) %collective-permute-start.9) | collective-permute-done | bytes 131104 | tf_op jit(solution)/shard_map/ppermute | solution.py:255
  64.2 10.1 %late.1 = (f32[3,64,512]{2,1,0:T(8,128)}, bf16[4,3,64,512]{3,2,1,0:T(8,128)(2,1)}, bf16[1024,768]{1,0:T(8,128)(2,1)}, bf16[256,768]{1,0:T(8,128)(2,1)}, bf16[256,256]{1,0:T(8,128)(2,1)}) custom-call(s32[2]{0:T(128)} %pad_add_fusion.place, bf16[256,512]{1,0:T(8,128)(2,1)} %copy-done.8, bf16[256,512]{1,0:T(8,128)(2,1)} %copy-done.13, ...), custom_call_target="tpu_custom_call" | custom-call | flops 11000000512 | bytes 6291456 | tf_op jit(solution)/shard_map/late/pallas_call | solution.py:357
  74.3 12.1 %all-to-all-start.1 = ((bf16[16,64,768]{2,1,0:T(8,128)(2,1)}), bf16[16,64,768]{2,1,0:T(8,128)(2,1)}, u32[]{:S(2)}, u32[]{:S(2)}) async-start(bf16[16,64,768]{2,1,0:T(8,128)(2,1)} %bitcast.67), calls=%async_computation.1 | async-start | bytes 3145728 | tf_op jit(solution)/shard_map/all_to_all | solution.py:391
  86.6 3.6 %collective-permute-start.21 = (bf16[3,64,512]{2,1,0:T(8,128)(2,1)S(1)}, bf16[3,64,512]{2,1,0:T(8,128)(2,1)S(1)}, u32[]{:S(2)}, u32[]{:S(2)}) collective-permute-start(bf16[3,64,512]{2,1,0:T(8,128)(2,1)S(1)} %get-tuple-element.41), channel_id=1, source_target_pairs={{0,192},{32,224},{64,0},{96,32},{128,64},{160,96},{192,128},{224,1... | collective-permute-start | bytes 589832 | tf_op jit(solution)/shard_map/ppermute | solution.py:255
  94.1 2.1 %collective-permute-start.23 = (bf16[2,128,1024]{2,1,0:T(8,128)(2,1)}, bf16[2,128,1024]{2,1,0:T(8,128)(2,1)}, u32[]{:S(2)}, u32[]{:S(2)}) collective-permute-start(bf16[2,128,1024]{2,1,0:T(8,128)(2,1)} %fusion.3), channel_id=1, source_target_pairs={{0,32},{32,0},{64,96},{96,64},{128,160},{160,128},{192,224},{224,1... | collective-permute-start | bytes 1572872 | tf_op jit(solution)/shard_map/ppermute | solution.py:250
  96.2 7.1 %collective-permute-done.20 = bf16[3,64,512]{2,1,0:T(8,128)(2,1)S(1)} collective-permute-done((bf16[3,64,512]{2,1,0:T(8,128)(2,1)S(1)}, bf16[3,64,512]{2,1,0:T(8,128)(2,1)S(1)}, u32[]{:S(2)}, u32[]{:S(2)}) %collective-permute-start.20) | collective-permute-done | bytes 196640 | tf_op jit(solution)/shard_map/ppermute | solution.py:255
  103.5 3.2 %collective-permute-start.22 = (f32[3,32,512]{2,1,0:T(8,128)S(1)}, f32[3,32,512]{2,1,0:T(8,128)S(1)}, u32[]{:S(2)}, u32[]{:S(2)}) collective-permute-start(f32[3,32,512]{2,1,0:T(8,128)S(1)} %get-tuple-element.48), channel_id=1, source_target_pairs={{0,32},{32,0},{64,96},{96,64},{128,160},{160,128},{192,224},{224,1... | collective-permute-start | bytes 589832 | tf_op jit(solution)/shard_map/ppermute | solution.py:250
  108.6 4.2 %collective-permute-start.15 = (bf16[32,768]{1,0:T(8,128)(2,1)S(1)}, bf16[32,768]{1,0:T(8,128)(2,1)S(1)}, u32[]{:S(2)}, u32[]{:S(2)}) collective-permute-start(bf16[32,768]{1,0:T(8,128)(2,1)S(1)} %select_convert_fusion), channel_id=1, source_target_pairs={{0,1},{1,0},{2,3},{3,2},{4,5},{5,4},{6,7},{7,6},{8,9},{9,8},{10,11... | collective-permute-start | bytes 147464 | tf_op jit(solution)/shard_map/ppermute | solution.py:269
  114.3 3.4 %collective-permute-start.18 = (bf16[32,768]{1,0:T(8,128)(2,1)S(1)}, bf16[32,768]{1,0:T(8,128)(2,1)S(1)}, u32[]{:S(2)}, u32[]{:S(2)}) collective-permute-start(bf16[32,768]{1,0:T(8,128)(2,1)S(1)} %add_convert_fusion), channel_id=1, source_target_pairs={{0,192},{32,224},{64,0},{96,32},{128,64},{160,96},{192,128},{224,1... | collective-permute-start | bytes 147464 | tf_op jit(solution)/shard_map/ppermute | solution.py:255
  119.0 1.8 %collective-permute-start.16 = (bf16[32,768]{1,0:T(8,128)(2,1)S(1)}, bf16[32,768]{1,0:T(8,128)(2,1)S(1)}, u32[]{:S(2)}, u32[]{:S(2)}) collective-permute-start(bf16[32,768]{1,0:T(8,128)(2,1)S(1)} %add_convert_fusion), channel_id=1, source_target_pairs={{0,64},{32,96},{64,128},{96,160},{128,192},{160,224},{192,0},{224,... | collective-permute-start | bytes 147464 | tf_op jit(solution)/shard_map/ppermute | solution.py:255
  120.8 2.0 %fusion.4 = bf16[1,2,128,1024]{3,2,1,0:T(8,128)(2,1)} fusion(bf16[2,128,1024]{2,1,0:T(8,128)(2,1)} %collective-permute-done.23, f32[1,256,1024]{2,1,0:T(8,128)S(1)} %convolution_bitcast_fusion, f32[1,256,1024]{2,1,0:T(8,128)S(1)} %convolution_bitcast_fusion.1), kind=kLoop, calls=%fused_computation.13 | loop fusion | flops 1048576 | bytes 3145728 | tf_op jit(solution)/shard_map/broadcast_in_dim | solution.py:423
  122.8 1.7 %collective-permute-done.17 = bf16[32,768]{1,0:T(8,128)(2,1)S(1)} collective-permute-done((bf16[32,768]{1,0:T(8,128)(2,1)S(1)}, bf16[32,768]{1,0:T(8,128)(2,1)S(1)}, u32[]{:S(2)}, u32[]{:S(2)}) %collective-permute-start.17) | collective-permute-done | bytes 49184 | tf_op jit(solution)/shard_map/ppermute | solution.py:255
  125.3 2.9 %collective-permute-start.24 = (f32[32,768]{1,0:T(8,128)S(1)}, f32[32,768]{1,0:T(8,128)S(1)}, u32[]{:S(2)}, u32[]{:S(2)}) collective-permute-start(f32[32,768]{1,0:T(8,128)S(1)} %convert_add_fusion.1), channel_id=1, source_target_pairs={{0,32},{32,0},{64,96},{96,64},{128,160},{160,128},{192,224},{224,1... | collective-permute-start | bytes 294920 | tf_op jit(solution)/shard_map/ppermute | solution.py:250
  (112 shorter events, 26.1 us)
Async XLA Ops:
  2.6 8.6 %collective-permute-start.1 = (bf16[272,1024]{1,0:T(8,128)(2,1)S(1)}, bf16[272,1024]{1,0:T(8,128)(2,1)S(1)}, u32[]{:S(2)}, u32[]{:S(2)}) collective-permute-start(bf16[272,1024]{1,0:T(8,128)(2,1)S(1)} %pad_maximum_fusion.1), channel_id=1, source_target_pairs={{0,32},{32,0},{64,96},{96,64},{128,160},{160,128},{192,224},{224,1... | collective-permute-start | bytes 1671176 | tf_op jit(solution)/shard_map/ppermute | solution.py:250
  6.1 19.0 %collective-permute-start.5 = (bf16[144,1024]{1,0:T(8,128)(2,1)S(1)}, bf16[144,1024]{1,0:T(8,128)(2,1)}, u32[]{:S(2)}, u32[]{:S(2)}) collective-permute-start(bf16[144,1024]{1,0:T(8,128)(2,1)S(1)} %pad_maximum_fusion.2.refs_0_.refs_11_), channel_id=1, source_target_pairs={{0,192},{32,224},{64,0},{96,32},{128,64},{160,96},{192,128},{224,1... | collective-permute-start | bytes 884744 | tf_op jit(solution)/shard_map/ppermute | solution.py:255
  11.1 18.8 %collective-permute-start.3 = (bf16[144,1024]{1,0:T(8,128)(2,1)S(1)}, bf16[144,1024]{1,0:T(8,128)(2,1)}, u32[]{:S(2)}, u32[]{:S(2)}) collective-permute-start(bf16[144,1024]{1,0:T(8,128)(2,1)S(1)} %pad_maximum_fusion.2.refs_0_.refs_11_), channel_id=1, source_target_pairs={{0,64},{32,96},{64,128},{96,160},{128,192},{160,224},{192,0},{224,... | collective-permute-start | bytes 884744 | tf_op jit(solution)/shard_map/ppermute | solution.py:255
  12.5 30.6 %all-to-all-start = ((bf16[16,64,768]{2,1,0:T(8,128)(2,1)}), bf16[16,64,768]{2,1,0:T(8,128)(2,1)S(1)}, u32[]{:S(2)}, u32[]{:S(2)}) async-start(bf16[16,64,768]{2,1,0:T(8,128)(2,1)} %broadcast_in_dim.11), calls=%async_computation | async-start | bytes 3145728 | tf_op jit(solution)/shard_map/all_to_all | solution.py:293
  19.4 11.5 %collective-permute-start.2 = (bf16[2,128,256]{2,1,0:T(8,128)(2,1)S(1)}, bf16[2,128,256]{2,1,0:T(8,128)(2,1)S(1)}, u32[]{:S(2)}, u32[]{:S(2)}) collective-permute-start(bf16[2,128,256]{2,1,0:T(8,128)(2,1)S(1)} %select_bitcast_fusion.2), channel_id=1, source_target_pairs={{0,32},{32,0},{64,96},{96,64},{128,160},{160,128},{192,224},{224,1... | collective-permute-start | bytes 393224 | tf_op jit(solution)/shard_map/ppermute | solution.py:250
  26.0 9.7 %collective-permute-start.6 = (bf16[144,512]{1,0:T(8,128)(2,1)S(1)}, bf16[144,512]{1,0:T(8,128)(2,1)S(1)}, u32[]{:S(2)}, u32[]{:S(2)}) collective-permute-start(bf16[144,512]{1,0:T(8,128)(2,1)S(1)} %slice.162), channel_id=1, source_target_pairs={{0,192},{32,224},{64,0},{96,32},{128,64},{160,96},{192,128},{224,1... | collective-permute-start | bytes 442376 | tf_op jit(solution)/shard_map/ppermute | solution.py:255
  30.8 10.1 %collective-permute-start.4 = (bf16[144,512]{1,0:T(8,128)(2,1)S(1)}, bf16[144,512]{1,0:T(8,128)(2,1)}, u32[]{:S(2)}, u32[]{:S(2)}) collective-permute-start(bf16[144,512]{1,0:T(8,128)(2,1)S(1)} %slice.161), channel_id=1, source_target_pairs={{0,64},{32,96},{64,128},{96,160},{128,192},{160,224},{192,0},{224,... | collective-permute-start | bytes 442376 | tf_op jit(solution)/shard_map/ppermute | solution.py:255
  31.6 14.3 %collective-permute-start.12 = (bf16[144,1024]{1,0:T(8,128)(2,1)}, bf16[144,1024]{1,0:T(8,128)(2,1)S(1)}, u32[]{:S(2)}, u32[]{:S(2)}) collective-permute-start(bf16[144,1024]{1,0:T(8,128)(2,1)} %collective-permute-done.5.refs_4_), channel_id=1, source_target_pairs={{0,32},{32,0},{64,96},{96,64},{128,160},{160,128},{192,224},{224,1... | collective-permute-start | bytes 884744 | tf_op jit(solution)/shard_map/ppermute | solution.py:250
  32.0 13.9 %collective-permute-start.11 = (bf16[144,1024]{1,0:T(8,128)(2,1)}, bf16[144,1024]{1,0:T(8,128)(2,1)}, u32[]{:S(2)}, u32[]{:S(2)}) collective-permute-start(bf16[144,1024]{1,0:T(8,128)(2,1)} %collective-permute-done.3.refs_2_), channel_id=1, source_target_pairs={{0,32},{32,0},{64,96},{96,64},{128,160},{160,128},{192,224},{224,1... | collective-permute-start | bytes 884744 | tf_op jit(solution)/shard_map/ppermute | solution.py:250
  35.6 8.3 %collective-permute-start.14 = (bf16[144,512]{1,0:T(8,128)(2,1)S(1)}, bf16[144,512]{1,0:T(8,128)(2,1)}, u32[]{:S(2)}, u32[]{:S(2)}) collective-permute-start(bf16[144,512]{1,0:T(8,128)(2,1)S(1)} %collective-permute-done.6.refs_7_), channel_id=1, source_target_pairs={{0,32},{32,0},{64,96},{96,64},{128,160},{160,128},{192,224},{224,1... | collective-permute-start | bytes 442376 | tf_op jit(solution)/shard_map/ppermute | solution.py:250
  43.5 10.9 %collective-permute-start.8 = (bf16[256,512]{1,0:T(8,128)(2,1)S(1)}, bf16[256,512]{1,0:T(8,128)(2,1)S(1)}, u32[]{:S(2)}, u32[]{:S(2)}) collective-permute-start(bf16[256,512]{1,0:T(8,128)(2,1)S(1)} %maximum_maximum_fusion.refs_0_), channel_id=1, source_target_pairs={{0,192},{32,224},{64,0},{96,32},{128,64},{160,96},{192,128},{224,1... | collective-permute-start | bytes 786440 | tf_op jit(solution)/shard_map/ppermute | solution.py:255
  44.0 12.2 %collective-permute-start.7 = (bf16[256,512]{1,0:T(8,128)(2,1)S(1)}, bf16[256,512]{1,0:T(8,128)(2,1)S(1)}, u32[]{:S(2)}, u32[]{:S(2)}) collective-permute-start(bf16[256,512]{1,0:T(8,128)(2,1)S(1)} %maximum_maximum_fusion.refs_0_), channel_id=1, source_target_pairs={{0,64},{32,96},{64,128},{96,160},{128,192},{160,224},{192,0},{224,... | collective-permute-start | bytes 786440 | tf_op jit(solution)/shard_map/ppermute | solution.py:255
  54.4 6.9 %collective-permute-start.10 = (bf16[256,256]{1,0:T(8,128)(2,1)S(1)}, bf16[256,256]{1,0:T(8,128)(2,1)S(1)}, u32[]{:S(2)}, u32[]{:S(2)}) collective-permute-start(bf16[256,256]{1,0:T(8,128)(2,1)S(1)} %slice.164), channel_id=1, source_target_pairs={{0,192},{32,224},{64,0},{96,32},{128,64},{160,96},{192,128},{224,1... | collective-permute-start | bytes 393224 | tf_op jit(solution)/shard_map/ppermute | solution.py:255
  56.1 7.4 %collective-permute-start.9 = (bf16[256,256]{1,0:T(8,128)(2,1)S(1)}, bf16[256,256]{1,0:T(8,128)(2,1)S(1)}, u32[]{:S(2)}, u32[]{:S(2)}) collective-permute-start(bf16[256,256]{1,0:T(8,128)(2,1)S(1)} %slice.163), channel_id=1, source_target_pairs={{0,64},{32,96},{64,128},{96,160},{128,192},{160,224},{192,0},{224,... | collective-permute-start | bytes 393224 | tf_op jit(solution)/shard_map/ppermute | solution.py:255
  74.3 32.6 %all-to-all-start.1 = ((bf16[16,64,768]{2,1,0:T(8,128)(2,1)}), bf16[16,64,768]{2,1,0:T(8,128)(2,1)}, u32[]{:S(2)}, u32[]{:S(2)}) async-start(bf16[16,64,768]{2,1,0:T(8,128)(2,1)} %bitcast.67), calls=%async_computation.1 | async-start | bytes 3145728 | tf_op jit(solution)/shard_map/all_to_all | solution.py:391
  86.5 9.7 %collective-permute-start.19 = (bf16[3,64,512]{2,1,0:T(8,128)(2,1)S(1)}, bf16[3,64,512]{2,1,0:T(8,128)(2,1)S(1)}, u32[]{:S(2)}, u32[]{:S(2)}) collective-permute-start(bf16[3,64,512]{2,1,0:T(8,128)(2,1)S(1)} %get-tuple-element.40), channel_id=1, source_target_pairs={{0,64},{32,96},{64,128},{96,160},{128,192},{160,224},{192,0},{224,... | collective-permute-start | bytes 589832 | tf_op jit(solution)/shard_map/ppermute | solution.py:255
  86.6 9.6 %collective-permute-start.21 = (bf16[3,64,512]{2,1,0:T(8,128)(2,1)S(1)}, bf16[3,64,512]{2,1,0:T(8,128)(2,1)S(1)}, u32[]{:S(2)}, u32[]{:S(2)}) collective-permute-start(bf16[3,64,512]{2,1,0:T(8,128)(2,1)S(1)} %get-tuple-element.41), channel_id=1, source_target_pairs={{0,192},{32,224},{64,0},{96,32},{128,64},{160,96},{192,128},{224,1... | collective-permute-start | bytes 589832 | tf_op jit(solution)/shard_map/ppermute | solution.py:255
  90.2 13.2 %collective-permute-start.20 = (bf16[3,64,512]{2,1,0:T(8,128)(2,1)S(1)}, bf16[3,64,512]{2,1,0:T(8,128)(2,1)S(1)}, u32[]{:S(2)}, u32[]{:S(2)}) collective-permute-start(bf16[3,64,512]{2,1,0:T(8,128)(2,1)S(1)} %get-tuple-element.42), channel_id=1, source_target_pairs={{0,128},{32,160},{64,192},{96,224},{128,0},{160,32},{192,64},{224,... | collective-permute-start | bytes 589832 | tf_op jit(solution)/shard_map/ppermute | solution.py:255
  94.1 26.8 %collective-permute-start.23 = (bf16[2,128,1024]{2,1,0:T(8,128)(2,1)}, bf16[2,128,1024]{2,1,0:T(8,128)(2,1)}, u32[]{:S(2)}, u32[]{:S(2)}) collective-permute-start(bf16[2,128,1024]{2,1,0:T(8,128)(2,1)} %fusion.3), channel_id=1, source_target_pairs={{0,32},{32,0},{64,96},{96,64},{128,160},{160,128},{192,224},{224,1... | collective-permute-start | bytes 1572872 | tf_op jit(solution)/shard_map/ppermute | solution.py:250
  103.5 9.3 %collective-permute-start.22 = (f32[3,32,512]{2,1,0:T(8,128)S(1)}, f32[3,32,512]{2,1,0:T(8,128)S(1)}, u32[]{:S(2)}, u32[]{:S(2)}) collective-permute-start(f32[3,32,512]{2,1,0:T(8,128)S(1)} %get-tuple-element.48), channel_id=1, source_target_pairs={{0,32},{32,0},{64,96},{96,64},{128,160},{160,128},{192,224},{224,1... | collective-permute-start | bytes 589832 | tf_op jit(solution)/shard_map/ppermute | solution.py:250
  108.6 5.7 %collective-permute-start.15 = (bf16[32,768]{1,0:T(8,128)(2,1)S(1)}, bf16[32,768]{1,0:T(8,128)(2,1)S(1)}, u32[]{:S(2)}, u32[]{:S(2)}) collective-permute-start(bf16[32,768]{1,0:T(8,128)(2,1)S(1)} %select_convert_fusion), channel_id=1, source_target_pairs={{0,1},{1,0},{2,3},{3,2},{4,5},{5,4},{6,7},{7,6},{8,9},{9,8},{10,11... | collective-permute-start | bytes 147464 | tf_op jit(solution)/shard_map/ppermute | solution.py:269
  114.3 8.5 %collective-permute-start.18 = (bf16[32,768]{1,0:T(8,128)(2,1)S(1)}, bf16[32,768]{1,0:T(8,128)(2,1)S(1)}, u32[]{:S(2)}, u32[]{:S(2)}) collective-permute-start(bf16[32,768]{1,0:T(8,128)(2,1)S(1)} %add_convert_fusion), channel_id=1, source_target_pairs={{0,192},{32,224},{64,0},{96,32},{128,64},{160,96},{192,128},{224,1... | collective-permute-start | bytes 147464 | tf_op jit(solution)/shard_map/ppermute | solution.py:255
  117.7 6.9 %collective-permute-start.17 = (bf16[32,768]{1,0:T(8,128)(2,1)S(1)}, bf16[32,768]{1,0:T(8,128)(2,1)S(1)}, u32[]{:S(2)}, u32[]{:S(2)}) collective-permute-start(bf16[32,768]{1,0:T(8,128)(2,1)S(1)} %add_convert_fusion), channel_id=1, source_target_pairs={{0,128},{32,160},{64,192},{96,224},{128,0},{160,32},{192,64},{224,... | collective-permute-start | bytes 147464 | tf_op jit(solution)/shard_map/ppermute | solution.py:255
  119.0 6.2 %collective-permute-start.16 = (bf16[32,768]{1,0:T(8,128)(2,1)S(1)}, bf16[32,768]{1,0:T(8,128)(2,1)S(1)}, u32[]{:S(2)}, u32[]{:S(2)}) collective-permute-start(bf16[32,768]{1,0:T(8,128)(2,1)S(1)} %add_convert_fusion), channel_id=1, source_target_pairs={{0,64},{32,96},{64,128},{96,160},{128,192},{160,224},{192,0},{224,... | collective-permute-start | bytes 147464 | tf_op jit(solution)/shard_map/ppermute | solution.py:255
  (21 other events, 175.3 us)

commit v4 on v3

--- a/solution.py
+++ b/solution.py
@@ -279,7 +279,6 @@
         jnp.concatenate([proj_mine, proj_pair], axis=0),
         jnp.concatenate([proj_pair, proj_mine], axis=0),
     )
-    own_state = jnp.where(core == 0, state[0, 0], state[0, 1])
 
     tok = tokens[0]
     half_rows = rows // 2
@@ -311,6 +310,8 @@
     pieces = [packed, packed_mate, ahead, to_mate(ahead), behind, to_mate(behind)]
     pieces += [far_low, far_high, to_mate(far_low), to_mate(far_high)]
 
+    state, ahead = lax.optimization_barrier((state, ahead))
+    own_state = jnp.where(core == 0, state[0, 0], state[0, 1])
     second = jnp.concatenate([tok[1], tok1_mate], axis=0)
     query1 = jnp.dot(second, whole[:, :dim], preferred_element_type=F32).astype(BF)
     late_in = jnp.concatenate([query1, jnp.concatenate([cot[1], cot_mate[1]], axis=0)], axis=1)

time: 131 us -> 128 us (0.977)
  waiting for transfers between devices: 21.7 us -> 15.6 us
  starting transfers between devices: 62.1 us -> 65.8 us
    ppermute x14, starting transfers between devices: 24.2 us -> 32.4 us  [along(): lax.ppermute(value, 'seq', [(i, (i // CORES + hop) % groups * CORES + i %...]
    ppermute x14, waiting for transfers between devices: 19.8 us -> 13.4 us  [along(): lax.ppermute(value, 'seq', [(i, (i // CORES + hop) % groups * CORES + i %...]
    all_to_all x1, starting transfers between devices: 12.1 us -> 7.48 us  [on_device(): lax.all_to_all(dproj.reshape(plane, 2 * owned, 3 * dim), 'fsdp', 0, 0, ax...]
where the time goes in v4:
time: 128 us
  starting transfers between devices  65.8 us (51%)
  Pallas kernels  22.2 us (17%)
  waiting for transfers between devices  15.6 us (12%)
  other arithmetic  10.5 us (8%)
  local copies, waits for them, and re-layouts  9.35 us (7%)
  matrix products  3.26 us (3%)
    ppermute x14, starting transfers between devices, along(): lax.ppermute(value, 'seq', [(i, (i // CORES + hop) % groups * CORES + i %...  32.4 us
    ppermute x9, starting transfers between devices, to_mate(): lax.ppermute(value, 'seq', [(i, i // CORES * CORES + (i + 1) % CORES) for...  15.2 us
    ppermute x14, waiting for transfers between devices, along(): lax.ppermute(value, 'seq', [(i, (i // CORES + hop) % groups * CORES + i %...  13.4 us
    pallas_call x1, Pallas kernels, on_device(): pl.pallas_call(partial(late_kernel, groups, rows), out_shape=(shape((3, s...  10.1 us
    pallas_call x1, Pallas kernels, on_device(): pl.pallas_call(partial(update_kernel, groups, rows), out_shape=(shape((3,...  7.75 us
    all_to_all x1, starting transfers between devices, on_device(): lax.all_to_all(dproj.reshape(plane, 2 * owned, 3 * dim), 'fsdp', 0, 0, ax...  7.48 us
    all_to_all x1, starting transfers between devices, on_device(): lax.all_to_all(jnp.broadcast_to(both, (plane, 2 * owned, 3 * dim)), 'fsdp...  6.89 us
    pallas_call x1, Pallas kernels, on_device(): pl.pallas_call(early_kernel, out_shape=(shape((3, dim, hid), F32), shape(...  4.36 us
  transfers between devices with their start and end apart: 27, of which 9 were waited for; matrix products, arithmetic and copies ran while one was open for 15% of the time, Pallas kernels for 9%

profile of v4, /device:TPU:1, one launch (start us, length us, event | category | flops | bytes accessed | tf_op | source)
XLA Modules:
  0.0 127.8 jit_solution(14904096270549669177)
XLA Ops:
  2.6 3.3 %collective-permute-start.1 = (bf16[272,1024]{1,0:T(8,128)(2,1)S(1)}, bf16[272,1024]{1,0:T(8,128)(2,1)S(1)}, u32[]{:S(2)}, u32[]{:S(2)}) collective-permute-start(bf16[272,1024]{1,0:T(8,128)(2,1)S(1)} %pad_maximum_fusion.1), channel_id=1, source_target_pairs={{0,32},{32,0},{64,96},{96,64},{128,160},{160,128},{192,224},{224,1... | collective-permute-start | bytes 1671176 | tf_op jit(solution)/shard_map/ppermute | solution.py:250
  6.1 5.1 %collective-permute-start.5 = (bf16[144,1024]{1,0:T(8,128)(2,1)S(1)}, bf16[144,1024]{1,0:T(8,128)(2,1)}, u32[]{:S(2)}, u32[]{:S(2)}) collective-permute-start(bf16[144,1024]{1,0:T(8,128)(2,1)S(1)} %pad_maximum_fusion.2.refs_0_.refs_11_), channel_id=1, source_target_pairs={{0,192},{32,224},{64,0},{96,32},{128,64},{160,96},{192,128},{224,1... | collective-permute-start | bytes 884744 | tf_op jit(solution)/shard_map/ppermute | solution.py:255
  12.5 6.9 %all-to-all-start = ((bf16[16,64,768]{2,1,0:T(8,128)(2,1)}), bf16[16,64,768]{2,1,0:T(8,128)(2,1)S(1)}, u32[]{:S(2)}, u32[]{:S(2)}) async-start(bf16[16,64,768]{2,1,0:T(8,128)(2,1)} %broadcast_in_dim.11), calls=%async_computation | async-start | bytes 3145728 | tf_op jit(solution)/shard_map/all_to_all | solution.py:292
  23.5 3.7 %collective-permute-start.6 = (bf16[144,512]{1,0:T(8,128)(2,1)S(1)}, bf16[144,512]{1,0:T(8,128)(2,1)S(1)}, u32[]{:S(2)}, u32[]{:S(2)}) collective-permute-start(bf16[144,512]{1,0:T(8,128)(2,1)S(1)} %slice.162), channel_id=1, source_target_pairs={{0,192},{32,224},{64,0},{96,32},{128,64},{160,96},{192,128},{224,1... | collective-permute-start | bytes 442376 | tf_op jit(solution)/shard_map/ppermute | solution.py:255
  28.2 3.4 %select_bitcast_fusion.refs_11_.state.refs_6_ = f32[3,256,512]{2,1,0:T(8,128)} fusion(f32[1,2,3,256,512]{4,3,2,1,0:T(8,128)} %param.7, pred[]{:T(512)S(6)} %eq.5), kind=kLoop, calls=%fused_computation.3 | loop fusion | flops 393216 | bytes 4718593 | tf_op jit(solution)/shard_map/jit(_where)/select_n | solution.py:314
  31.6 3.1 %collective-permute-start.12 = (bf16[144,1024]{1,0:T(8,128)(2,1)}, bf16[144,1024]{1,0:T(8,128)(2,1)S(1)}, u32[]{:S(2)}, u32[]{:S(2)}) collective-permute-start(bf16[144,1024]{1,0:T(8,128)(2,1)} %collective-permute-done.5.refs_4_), channel_id=1, source_target_pairs={{0,32},{32,0},{64,96},{96,64},{128,160},{160,128},{192,224},{224,1... | collective-permute-start | bytes 884744 | tf_op jit(solution)/shard_map/ppermute | solution.py:250
  36.3 2.9 %collective-permute-start.13 = (bf16[144,512]{1,0:T(8,128)(2,1)S(1)}, bf16[144,512]{1,0:T(8,128)(2,1)}, u32[]{:S(2)}, u32[]{:S(2)}) collective-permute-start(bf16[144,512]{1,0:T(8,128)(2,1)S(1)} %collective-permute-done.4.refs_6_), channel_id=1, source_target_pairs={{0,32},{32,0},{64,96},{96,64},{128,160},{160,128},{192,224},{224,1... | collective-permute-start | bytes 442376 | tf_op jit(solution)/shard_map/ppermute | solution.py:250
  41.0 3.0 %collective-permute-start.8 = (bf16[256,512]{1,0:T(8,128)(2,1)S(1)}, bf16[256,512]{1,0:T(8,128)(2,1)S(1)}, u32[]{:S(2)}, u32[]{:S(2)}) collective-permute-start(bf16[256,512]{1,0:T(8,128)(2,1)S(1)} %maximum_maximum_fusion.refs_0_), channel_id=1, source_target_pairs={{0,192},{32,224},{64,0},{96,32},{128,64},{160,96},{192,128},{224,1... | collective-permute-start | bytes 786440 | tf_op jit(solution)/shard_map/ppermute | solution.py:255
  44.7 7.8 %update.1 = (bf16[3,256,512]{2,1,0:T(8,128)(2,1)}, bf16[256,512]{1,0:T(8,128)(2,1)}, f32[256,128]{1,0:T(8,128)}) custom-call(s32[1]{0:T(128)} %bitcast.1.head_ref, bf16[144,1024]{1,0:T(8,128)(2,1)} %copy-done.7, bf16[144,1024]{1,0:T(8,128)(2,1)} %slice.140.refs_1_.refs_12_, bf16[144,1024]{1,0:T(8,128)(2,1)} %collective-permute-done.3.refs_2_, ...), custom_call_target="tpu_custom_call" | custom-call | flops 8999999488 | bytes 6291456 | tf_op jit(solution)/shard_map/update/pallas_call | solution.py:337
  52.5 3.7 %collective-permute-start.10 = (bf16[256,256]{1,0:T(8,128)(2,1)S(1)}, bf16[256,256]{1,0:T(8,128)(2,1)S(1)}, u32[]{:S(2)}, u32[]{:S(2)}) collective-permute-start(bf16[256,256]{1,0:T(8,128)(2,1)S(1)} %slice.164), channel_id=1, source_target_pairs={{0,192},{32,224},{64,0},{96,32},{128,64},{160,96},{192,128},{224,1... | collective-permute-start | bytes 393224 | tf_op jit(solution)/shard_map/ppermute | solution.py:255
  56.3 4.4 %early.1 = (f32[3,256,512]{2,1,0:T(8,128)}, bf16[256,256]{1,0:T(8,128)(2,1)}) custom-call(bf16[1024,768]{1,0:T(8,128)(2,1)} %bitcast.64, f32[3,256,512]{2,1,0:T(8,128)} %select_bitcast_fusion.refs_11_.state.refs_6_, bf16[128,1024]{1,0:T(8,128)(2,1)} %copy-done.2, bf16[128,1024]{1,0:T(8,128)(2,1)} %get-tuple-element.45.tok_mate, ...), custom_call_target="tpu_custom_call" | custom-call | flops 4000000000 | bytes 6291456 | tf_op jit(solution)/shard_map/early/pallas_call | solution.py:326
  60.7 1.7 %collective-permute-done.9.refs_3_ = bf16[256,256]{1,0:T(8,128)(2,1)S(1)} collective-permute-done((bf16[256,256]{1,0:T(8,128)(2,1)S(1)}, bf16[256,256]{1,0:T(8,128)(2,1)S(1)}, u32[]{:S(2)}, u32[]{:S(2)}) %collective-permute-start.9) | collective-permute-done | bytes 131104 | tf_op jit(solution)/shard_map/ppermute | solution.py:255
  63.0 10.1 %late.1 = (f32[3,64,512]{2,1,0:T(8,128)}, bf16[4,3,64,512]{3,2,1,0:T(8,128)(2,1)}, bf16[1024,768]{1,0:T(8,128)(2,1)}, bf16[256,768]{1,0:T(8,128)(2,1)}, bf16[256,256]{1,0:T(8,128)(2,1)}) custom-call(s32[2]{0:T(128)} %pad_add_fusion.place, bf16[256,512]{1,0:T(8,128)(2,1)} %copy-done.8, bf16[256,512]{1,0:T(8,128)(2,1)} %copy-done.13, ...), custom_call_target="tpu_custom_call" | custom-call | flops 11000000512 | bytes 6291456 | tf_op jit(solution)/shard_map/late/pallas_call | solution.py:358
  73.2 7.5 %all-to-all-start.1 = ((bf16[16,64,768]{2,1,0:T(8,128)(2,1)}), bf16[16,64,768]{2,1,0:T(8,128)(2,1)}, u32[]{:S(2)}, u32[]{:S(2)}) async-start(bf16[16,64,768]{2,1,0:T(8,128)(2,1)} %bitcast.67), calls=%async_computation.1 | async-start | bytes 3145728 | tf_op jit(solution)/shard_map/all_to_all | solution.py:392
  80.7 3.3 %collective-permute-start.19 = (bf16[3,64,512]{2,1,0:T(8,128)(2,1)S(1)}, bf16[3,64,512]{2,1,0:T(8,128)(2,1)S(1)}, u32[]{:S(2)}, u32[]{:S(2)}) collective-permute-start(bf16[3,64,512]{2,1,0:T(8,128)(2,1)S(1)} %get-tuple-element.42), channel_id=1, source_target_pairs={{0,64},{32,96},{64,128},{96,160},{128,192},{160,224},{192,0},{224,... | collective-permute-start | bytes 589832 | tf_op jit(solution)/shard_map/ppermute | solution.py:255
  84.4 7.4 %collective-permute-start.20 = (bf16[3,64,512]{2,1,0:T(8,128)(2,1)S(1)}, bf16[3,64,512]{2,1,0:T(8,128)(2,1)S(1)}, u32[]{:S(2)}, u32[]{:S(2)}) collective-permute-start(bf16[3,64,512]{2,1,0:T(8,128)(2,1)S(1)} %get-tuple-element.44), channel_id=1, source_target_pairs={{0,128},{32,160},{64,192},{96,224},{128,0},{160,32},{192,64},{224,... | collective-permute-start | bytes 589832 | tf_op jit(solution)/shard_map/ppermute | solution.py:255
  95.6 2.1 %collective-permute-start.23 = (bf16[2,128,1024]{2,1,0:T(8,128)(2,1)}, bf16[2,128,1024]{2,1,0:T(8,128)(2,1)}, u32[]{:S(2)}, u32[]{:S(2)}) collective-permute-start(bf16[2,128,1024]{2,1,0:T(8,128)(2,1)} %fusion.3), channel_id=1, source_target_pairs={{0,32},{32,0},{64,96},{96,64},{128,160},{160,128},{192,224},{224,1... | collective-permute-start | bytes 1572872 | tf_op jit(solution)/shard_map/ppermute | solution.py:250
  97.7 5.6 %collective-permute-done.21 = bf16[3,64,512]{2,1,0:T(8,128)(2,1)S(1)} collective-permute-done((bf16[3,64,512]{2,1,0:T(8,128)(2,1)S(1)}, bf16[3,64,512]{2,1,0:T(8,128)(2,1)S(1)}, u32[]{:S(2)}, u32[]{:S(2)}) %collective-permute-start.21) | collective-permute-done | bytes 196640 | tf_op jit(solution)/shard_map/ppermute | solution.py:255
  106.4 3.8 %collective-permute-start.15 = (bf16[32,768]{1,0:T(8,128)(2,1)S(1)}, bf16[32,768]{1,0:T(8,128)(2,1)S(1)}, u32[]{:S(2)}, u32[]{:S(2)}) collective-permute-start(bf16[32,768]{1,0:T(8,128)(2,1)S(1)} %select_convert_fusion), channel_id=1, source_target_pairs={{0,1},{1,0},{2,3},{3,2},{4,5},{5,4},{6,7},{7,6},{8,9},{9,8},{10,11... | collective-permute-start | bytes 147464 | tf_op jit(solution)/shard_map/ppermute | solution.py:269
  112.3 2.6 %collective-permute-start.18 = (bf16[32,768]{1,0:T(8,128)(2,1)S(1)}, bf16[32,768]{1,0:T(8,128)(2,1)S(1)}, u32[]{:S(2)}, u32[]{:S(2)}) collective-permute-start(bf16[32,768]{1,0:T(8,128)(2,1)S(1)} %add_convert_fusion), channel_id=1, source_target_pairs={{0,192},{32,224},{64,0},{96,32},{128,64},{160,96},{192,128},{224,1... | collective-permute-start | bytes 147464 | tf_op jit(solution)/shard_map/ppermute | solution.py:255
  114.9 3.1 %collective-permute-start.17 = (bf16[32,768]{1,0:T(8,128)(2,1)S(1)}, bf16[32,768]{1,0:T(8,128)(2,1)S(1)}, u32[]{:S(2)}, u32[]{:S(2)}) collective-permute-start(bf16[32,768]{1,0:T(8,128)(2,1)S(1)} %add_convert_fusion), channel_id=1, source_target_pairs={{0,128},{32,160},{64,192},{96,224},{128,0},{160,32},{192,64},{224,... | collective-permute-start | bytes 147464 | tf_op jit(solution)/shard_map/ppermute | solution.py:255
  118.0 2.0 %fusion.4 = bf16[1,2,128,1024]{3,2,1,0:T(8,128)(2,1)} fusion(bf16[2,128,1024]{2,1,0:T(8,128)(2,1)} %collective-permute-done.23, f32[1,256,1024]{2,1,0:T(8,128)S(1)} %convolution_bitcast_fusion, f32[1,256,1024]{2,1,0:T(8,128)S(1)} %convolution_bitcast_fusion.1), kind=kLoop, calls=%fused_computation.13 | loop fusion | flops 1048576 | bytes 3145728 | tf_op jit(solution)/shard_map/broadcast_in_dim | solution.py:424
  120.0 2.2 %collective-permute-done.17 = bf16[32,768]{1,0:T(8,128)(2,1)S(1)} collective-permute-done((bf16[32,768]{1,0:T(8,128)(2,1)S(1)}, bf16[32,768]{1,0:T(8,128)(2,1)S(1)}, u32[]{:S(2)}, u32[]{:S(2)}) %collective-permute-start.17) | collective-permute-done | bytes 49184 | tf_op jit(solution)/shard_map/ppermute | solution.py:255
  122.2 2.1 %collective-permute-done.16 = bf16[32,768]{1,0:T(8,128)(2,1)S(1)} collective-permute-done((bf16[32,768]{1,0:T(8,128)(2,1)S(1)}, bf16[32,768]{1,0:T(8,128)(2,1)S(1)}, u32[]{:S(2)}, u32[]{:S(2)}) %collective-permute-start.16) | collective-permute-done | bytes 49184 | tf_op jit(solution)/shard_map/ppermute | solution.py:255
  (114 shorter events, 26.1 us)
Async XLA Ops:
  2.6 8.6 %collective-permute-start.1 = (bf16[272,1024]{1,0:T(8,128)(2,1)S(1)}, bf16[272,1024]{1,0:T(8,128)(2,1)S(1)}, u32[]{:S(2)}, u32[]{:S(2)}) collective-permute-start(bf16[272,1024]{1,0:T(8,128)(2,1)S(1)} %pad_maximum_fusion.1), channel_id=1, source_target_pairs={{0,32},{32,0},{64,96},{96,64},{128,160},{160,128},{192,224},{224,1... | collective-permute-start | bytes 1671176 | tf_op jit(solution)/shard_map/ppermute | solution.py:250
  6.1 16.5 %collective-permute-start.5 = (bf16[144,1024]{1,0:T(8,128)(2,1)S(1)}, bf16[144,1024]{1,0:T(8,128)(2,1)}, u32[]{:S(2)}, u32[]{:S(2)}) collective-permute-start(bf16[144,1024]{1,0:T(8,128)(2,1)S(1)} %pad_maximum_fusion.2.refs_0_.refs_11_), channel_id=1, source_target_pairs={{0,192},{32,224},{64,0},{96,32},{128,64},{160,96},{192,128},{224,1... | collective-permute-start | bytes 884744 | tf_op jit(solution)/shard_map/ppermute | solution.py:255
  11.1 16.1 %collective-permute-start.3 = (bf16[144,1024]{1,0:T(8,128)(2,1)S(1)}, bf16[144,1024]{1,0:T(8,128)(2,1)}, u32[]{:S(2)}, u32[]{:S(2)}) collective-permute-start(bf16[144,1024]{1,0:T(8,128)(2,1)S(1)} %pad_maximum_fusion.2.refs_0_.refs_11_), channel_id=1, source_target_pairs={{0,64},{32,96},{64,128},{96,160},{128,192},{160,224},{192,0},{224,... | collective-permute-start | bytes 884744 | tf_op jit(solution)/shard_map/ppermute | solution.py:255
  12.5 28.1 %all-to-all-start = ((bf16[16,64,768]{2,1,0:T(8,128)(2,1)}), bf16[16,64,768]{2,1,0:T(8,128)(2,1)S(1)}, u32[]{:S(2)}, u32[]{:S(2)}) async-start(bf16[16,64,768]{2,1,0:T(8,128)(2,1)} %broadcast_in_dim.11), calls=%async_computation | async-start | bytes 3145728 | tf_op jit(solution)/shard_map/all_to_all | solution.py:292
  23.5 11.3 %collective-permute-start.6 = (bf16[144,512]{1,0:T(8,128)(2,1)S(1)}, bf16[144,512]{1,0:T(8,128)(2,1)S(1)}, u32[]{:S(2)}, u32[]{:S(2)}) collective-permute-start(bf16[144,512]{1,0:T(8,128)(2,1)S(1)} %slice.162), channel_id=1, source_target_pairs={{0,192},{32,224},{64,0},{96,32},{128,64},{160,96},{192,128},{224,1... | collective-permute-start | bytes 442376 | tf_op jit(solution)/shard_map/ppermute | solution.py:255
  28.2 8.1 %collective-permute-start.4 = (bf16[144,512]{1,0:T(8,128)(2,1)S(1)}, bf16[144,512]{1,0:T(8,128)(2,1)S(1)}, u32[]{:S(2)}, u32[]{:S(2)}) collective-permute-start(bf16[144,512]{1,0:T(8,128)(2,1)S(1)} %slice.161), channel_id=1, source_target_pairs={{0,64},{32,96},{64,128},{96,160},{128,192},{160,224},{192,0},{224,... | collective-permute-start | bytes 442376 | tf_op jit(solution)/shard_map/ppermute | solution.py:255
  31.6 12.4 %collective-permute-start.12 = (bf16[144,1024]{1,0:T(8,128)(2,1)}, bf16[144,1024]{1,0:T(8,128)(2,1)S(1)}, u32[]{:S(2)}, u32[]{:S(2)}) collective-permute-start(bf16[144,1024]{1,0:T(8,128)(2,1)} %collective-permute-done.5.refs_4_), channel_id=1, source_target_pairs={{0,32},{32,0},{64,96},{96,64},{128,160},{160,128},{192,224},{224,1... | collective-permute-start | bytes 884744 | tf_op jit(solution)/shard_map/ppermute | solution.py:250
  34.8 9.3 %collective-permute-start.11 = (bf16[144,1024]{1,0:T(8,128)(2,1)}, bf16[144,1024]{1,0:T(8,128)(2,1)}, u32[]{:S(2)}, u32[]{:S(2)}) collective-permute-start(bf16[144,1024]{1,0:T(8,128)(2,1)} %collective-permute-done.3.refs_2_), channel_id=1, source_target_pairs={{0,32},{32,0},{64,96},{96,64},{128,160},{160,128},{192,224},{224,1... | collective-permute-start | bytes 884744 | tf_op jit(solution)/shard_map/ppermute | solution.py:250
  34.8 9.2 %collective-permute-start.14 = (bf16[144,512]{1,0:T(8,128)(2,1)S(1)}, bf16[144,512]{1,0:T(8,128)(2,1)}, u32[]{:S(2)}, u32[]{:S(2)}) collective-permute-start(bf16[144,512]{1,0:T(8,128)(2,1)S(1)} %collective-permute-done.6.refs_7_), channel_id=1, source_target_pairs={{0,32},{32,0},{64,96},{96,64},{128,160},{160,128},{192,224},{224,1... | collective-permute-start | bytes 442376 | tf_op jit(solution)/shard_map/ppermute | solution.py:250
  36.3 7.7 %collective-permute-start.13 = (bf16[144,512]{1,0:T(8,128)(2,1)S(1)}, bf16[144,512]{1,0:T(8,128)(2,1)}, u32[]{:S(2)}, u32[]{:S(2)}) collective-permute-start(bf16[144,512]{1,0:T(8,128)(2,1)S(1)} %collective-permute-done.4.refs_6_), channel_id=1, source_target_pairs={{0,32},{32,0},{64,96},{96,64},{128,160},{160,128},{192,224},{224,1... | collective-permute-start | bytes 442376 | tf_op jit(solution)/shard_map/ppermute | solution.py:250
  41.0 11.5 %collective-permute-start.8 = (bf16[256,512]{1,0:T(8,128)(2,1)S(1)}, bf16[256,512]{1,0:T(8,128)(2,1)S(1)}, u32[]{:S(2)}, u32[]{:S(2)}) collective-permute-start(bf16[256,512]{1,0:T(8,128)(2,1)S(1)} %maximum_maximum_fusion.refs_0_), channel_id=1, source_target_pairs={{0,192},{32,224},{64,0},{96,32},{128,64},{160,96},{192,128},{224,1... | collective-permute-start | bytes 786440 | tf_op jit(solution)/shard_map/ppermute | solution.py:255
  44.0 12.2 %collective-permute-start.7 = (bf16[256,512]{1,0:T(8,128)(2,1)S(1)}, bf16[256,512]{1,0:T(8,128)(2,1)S(1)}, u32[]{:S(2)}, u32[]{:S(2)}) collective-permute-start(bf16[256,512]{1,0:T(8,128)(2,1)S(1)} %maximum_maximum_fusion.refs_0_), channel_id=1, source_target_pairs={{0,64},{32,96},{64,128},{96,160},{128,192},{160,224},{192,0},{224,... | collective-permute-start | bytes 786440 | tf_op jit(solution)/shard_map/ppermute | solution.py:255
  52.5 8.1 %collective-permute-start.10 = (bf16[256,256]{1,0:T(8,128)(2,1)S(1)}, bf16[256,256]{1,0:T(8,128)(2,1)S(1)}, u32[]{:S(2)}, u32[]{:S(2)}) collective-permute-start(bf16[256,256]{1,0:T(8,128)(2,1)S(1)} %slice.164), channel_id=1, source_target_pairs={{0,192},{32,224},{64,0},{96,32},{128,64},{160,96},{192,128},{224,1... | collective-permute-start | bytes 393224 | tf_op jit(solution)/shard_map/ppermute | solution.py:255
  56.2 6.2 %collective-permute-start.9 = (bf16[256,256]{1,0:T(8,128)(2,1)S(1)}, bf16[256,256]{1,0:T(8,128)(2,1)S(1)}, u32[]{:S(2)}, u32[]{:S(2)}) collective-permute-start(bf16[256,256]{1,0:T(8,128)(2,1)S(1)} %slice.163), channel_id=1, source_target_pairs={{0,64},{32,96},{64,128},{96,160},{128,192},{160,224},{192,0},{224,... | collective-permute-start | bytes 393224 | tf_op jit(solution)/shard_map/ppermute | solution.py:255
  73.2 31.6 %all-to-all-start.1 = ((bf16[16,64,768]{2,1,0:T(8,128)(2,1)}), bf16[16,64,768]{2,1,0:T(8,128)(2,1)}, u32[]{:S(2)}, u32[]{:S(2)}) async-start(bf16[16,64,768]{2,1,0:T(8,128)(2,1)} %bitcast.67), calls=%async_computation.1 | async-start | bytes 3145728 | tf_op jit(solution)/shard_map/all_to_all | solution.py:392
  80.7 17.0 %collective-permute-start.19 = (bf16[3,64,512]{2,1,0:T(8,128)(2,1)S(1)}, bf16[3,64,512]{2,1,0:T(8,128)(2,1)S(1)}, u32[]{:S(2)}, u32[]{:S(2)}) collective-permute-start(bf16[3,64,512]{2,1,0:T(8,128)(2,1)S(1)} %get-tuple-element.42), channel_id=1, source_target_pairs={{0,64},{32,96},{64,128},{96,160},{128,192},{160,224},{192,0},{224,... | collective-permute-start | bytes 589832 | tf_op jit(solution)/shard_map/ppermute | solution.py:255
  84.0 19.4 %collective-permute-start.21 = (bf16[3,64,512]{2,1,0:T(8,128)(2,1)S(1)}, bf16[3,64,512]{2,1,0:T(8,128)(2,1)S(1)}, u32[]{:S(2)}, u32[]{:S(2)}) collective-permute-start(bf16[3,64,512]{2,1,0:T(8,128)(2,1)S(1)} %get-tuple-element.43), channel_id=1, source_target_pairs={{0,192},{32,224},{64,0},{96,32},{128,64},{160,96},{192,128},{224,1... | collective-permute-start | bytes 589832 | tf_op jit(solution)/shard_map/ppermute | solution.py:255
  84.4 19.6 %collective-permute-start.20 = (bf16[3,64,512]{2,1,0:T(8,128)(2,1)S(1)}, bf16[3,64,512]{2,1,0:T(8,128)(2,1)S(1)}, u32[]{:S(2)}, u32[]{:S(2)}) collective-permute-start(bf16[3,64,512]{2,1,0:T(8,128)(2,1)S(1)} %get-tuple-element.44), channel_id=1, source_target_pairs={{0,128},{32,160},{64,192},{96,224},{128,0},{160,32},{192,64},{224,... | collective-permute-start | bytes 589832 | tf_op jit(solution)/shard_map/ppermute | solution.py:255
  95.6 22.4 %collective-permute-start.23 = (bf16[2,128,1024]{2,1,0:T(8,128)(2,1)}, bf16[2,128,1024]{2,1,0:T(8,128)(2,1)}, u32[]{:S(2)}, u32[]{:S(2)}) collective-permute-start(bf16[2,128,1024]{2,1,0:T(8,128)(2,1)} %fusion.3), channel_id=1, source_target_pairs={{0,32},{32,0},{64,96},{96,64},{128,160},{160,128},{192,224},{224,1... | collective-permute-start | bytes 1572872 | tf_op jit(solution)/shard_map/ppermute | solution.py:250
  104.2 6.0 %collective-permute-start.22 = (f32[3,32,512]{2,1,0:T(8,128)S(1)}, f32[3,32,512]{2,1,0:T(8,128)S(1)}, u32[]{:S(2)}, u32[]{:S(2)}) collective-permute-start(f32[3,32,512]{2,1,0:T(8,128)S(1)} %get-tuple-element.50), channel_id=1, source_target_pairs={{0,32},{32,0},{64,96},{96,64},{128,160},{160,128},{192,224},{224,1... | collective-permute-start | bytes 589832 | tf_op jit(solution)/shard_map/ppermute | solution.py:250
  106.4 5.9 %collective-permute-start.15 = (bf16[32,768]{1,0:T(8,128)(2,1)S(1)}, bf16[32,768]{1,0:T(8,128)(2,1)S(1)}, u32[]{:S(2)}, u32[]{:S(2)}) collective-permute-start(bf16[32,768]{1,0:T(8,128)(2,1)S(1)} %select_convert_fusion), channel_id=1, source_target_pairs={{0,1},{1,0},{2,3},{3,2},{4,5},{5,4},{6,7},{7,6},{8,9},{9,8},{10,11... | collective-permute-start | bytes 147464 | tf_op jit(solution)/shard_map/ppermute | solution.py:269
  112.3 7.7 %collective-permute-start.18 = (bf16[32,768]{1,0:T(8,128)(2,1)S(1)}, bf16[32,768]{1,0:T(8,128)(2,1)S(1)}, u32[]{:S(2)}, u32[]{:S(2)}) collective-permute-start(bf16[32,768]{1,0:T(8,128)(2,1)S(1)} %add_convert_fusion), channel_id=1, source_target_pairs={{0,192},{32,224},{64,0},{96,32},{128,64},{160,96},{192,128},{224,1... | collective-permute-start | bytes 147464 | tf_op jit(solution)/shard_map/ppermute | solution.py:255
  114.9 7.3 %collective-permute-start.17 = (bf16[32,768]{1,0:T(8,128)(2,1)S(1)}, bf16[32,768]{1,0:T(8,128)(2,1)S(1)}, u32[]{:S(2)}, u32[]{:S(2)}) collective-permute-start(bf16[32,768]{1,0:T(8,128)(2,1)S(1)} %add_convert_fusion), channel_id=1, source_target_pairs={{0,128},{32,160},{64,192},{96,224},{128,0},{160,32},{192,64},{224,... | collective-permute-start | bytes 147464 | tf_op jit(solution)/shard_map/ppermute | solution.py:255
  118.0 6.3 %collective-permute-start.16 = (bf16[32,768]{1,0:T(8,128)(2,1)S(1)}, bf16[32,768]{1,0:T(8,128)(2,1)S(1)}, u32[]{:S(2)}, u32[]{:S(2)}) collective-permute-start(bf16[32,768]{1,0:T(8,128)(2,1)S(1)} %add_convert_fusion), channel_id=1, source_target_pairs={{0,64},{32,96},{64,128},{96,160},{128,192},{160,224},{192,0},{224,... | collective-permute-start | bytes 147464 | tf_op jit(solution)/shard_map/ppermute | solution.py:255
  (22 other events, 178.3 us)
